TPU v7x, 512 devices: a whole 4x4x16 slice. The times are simulated.
512 devices in a mesh: dp: 32 (over z, core), tensor: 16 (over x, y).
Axes of the slice: x: 4, y: 4, z: 16, core: 2. Of those that a mesh axis runs over, the one named last changes fastest.
Arguments:
- hidden_acts: bfloat16 [12288, 28672], P('dp', 'tensor'), may hold values from -6 to 6
- out_grads: bfloat16 [12288, 8192], P('dp', 'tensor'), may hold values from -6 to 6
- query_left: bfloat16 [1024, 28672], P('dp', 'tensor'), may hold values from -10 to 10, as said below
- query_right: bfloat16 [1024, 8192], P('dp', 'tensor'), may hold values from -10 to 10, as said below
Outputs:
- influence: float32 [32, 12288], P(None, 'dp')
Inputs may be any that keep to these rules, and one draw needn't show every extreme that they name: `query_left`: rows q * 32 to q * 32 + 31 are the hidden-unit factors of query q. `query_right`: rows q * 32 to q * 32 + 31 are the model-width factors of query q.
All inputs are finite; a program needn't handle non-finite values.
Results may differ from a plain program's by a relative error of at most 0.0003.
Values may be sent and summed in bfloat16 or wider, within the bound.
No kernel may reach another device: no remote copies, remote signals or barrier semaphores. Data moves between devices by JAX's collectives and lax.ppermute only.
A program may use at most 64 MiB of HBM per device.

v0:
```python
import jax
import jax.numpy as jnp
from jax import lax
from jax.sharding import PartitionSpec as P

Q = 32
R = 32


epsilon = 1e-06


def contract(rows_here, factors):
    return jnp.einsum("tf,kf->tk", rows_here, factors, preferred_element_type=jnp.float32)


def own_gram(panel):
    factor_rows, columns = panel.shape
    blocks = panel.reshape(factor_rows // R, R, columns)
    return jnp.einsum("qrf,qsf->qrs", blocks, blocks, preferred_element_type=jnp.float32)


def on_device(hidden_acts, out_grads, query_left, query_right):
    tokens_here = hidden_acts.shape[0]
    left_terms = contract(hidden_acts, lax.all_gather(query_left, "dp", axis=0, tiled=True))
    right_terms = contract(out_grads, lax.all_gather(query_right, "dp", axis=0, tiled=True))
    gram_left, gram_right = lax.psum((own_gram(query_left), own_gram(query_right)), "tensor")
    own_norm = jnp.sqrt(jnp.sum(gram_left * gram_right, axis=(1, 2)) + epsilon)
    norms_gathered = lax.all_gather(own_norm, "dp", axis=0, tiled=True)
    left_summed, right_summed = lax.psum((left_terms, right_terms), "tensor")
    query_count = Q
    products = left_summed * right_summed
    scores = (
        jnp.sum(products.reshape(tokens_here, query_count, R), axis=2).T / norms_gathered[:, None]
    )
    return scores


def solution(mesh):
    placed = (P("dp", "tensor"), P("dp", "tensor"), P("dp", "tensor"), P("dp", "tensor"))
    return jax.shard_map(
        on_device, mesh=mesh, in_specs=placed, out_specs=P(None, "dp"), check_vma=False
    )
```

profile of v0, /device:TPU:1, one launch (start us, length us, event | category | flops | bytes accessed | tf_op | source)
XLA Modules:
  0.0 301.6 jit_solution(493716486032934919)
XLA Ops:
  6.5 0.0 copy-start
  6.5 0.0 all-gather.5.cloned.1.call-start
  6.5 0.7 all-gather.5.cloned.1.call-update
  7.3 0.0 all-gather.3.cloned.1.call-start
  7.3 0.7 all-gather.3.cloned.1.call-update
  8.0 0.0 all-reduce.5.cloned.1.call-start
  8.1 77.8 %all-gather.5.cloned.1.call-done = bf16[1024,512]{1,0:T(8,128)(2,1)} async-done(((bf16[32,512]{1,0:T(8,128)(2,1)}), bf16[1024,512]{1,0:T(8,128)(2,1)}) %all-gather.5.cloned.1.call-update) | async-done | bytes 1048592 | tf_op jit(solution)/shard_map/all_gather | solution.py:26
  85.9 3.1 %fusion.1 = f32[384,1024]{1,0:T(8,128)} fusion(bf16[384,512]{1,0:T(8,128)(2,1)} %param.5, bf16[1024,512]{1,0:T(8,128)(2,1)} %all-gather.5.cloned.1.call-done), kind=kOutput, calls=%fused_computation.6 | convolution fusion | flops 402653184 | bytes 3014656 | tf_op jit(solution)/shard_map/tf,kf->tk/dot_general | solution.py:14
  89.0 69.7 %all-gather.3.cloned.1.call-done = bf16[1024,1792]{1,0:T(8,128)(2,1)} async-done(((bf16[32,1792]{1,0:T(8,128)(2,1)}), bf16[1024,1792]{1,0:T(8,128)(2,1)}) %all-gather.3.cloned.1.call-update) | async-done | bytes 3670032 | tf_op jit(solution)/shard_map/all_gather | solution.py:25
  158.7 0.0 copy-done
  158.8 4.9 %fusion = f32[384,1024]{1,0:T(8,128)} fusion(bf16[384,1792]{1,0:T(8,128)(2,1)S(1)} %copy-done, bf16[1024,1792]{1,0:T(8,128)(2,1)} %all-gather.3.cloned.1.call-done), kind=kOutput, calls=%fused_computation.5 | convolution fusion | flops 1409286144 | bytes 6619136 | tf_op jit(solution)/shard_map/tf,kf->tk/dot_general | solution.py:14
  163.6 0.0 copy-start.2
  163.6 0.0 copy-start.1
  163.6 0.0 all-reduce.5.cloned.1.call-update
  163.6 0.7 copy-done.2
  164.4 0.1 convolution_bitcast_fusion
  164.5 0.0 copy-done.1
  164.5 0.1 convolution_bitcast_fusion.1
  164.7 60.8 %all-reduce.1 = (f32[1,32,32]{2,1,0:T(8,128)S(1)}, f32[1,32,32]{2,1,0:T(8,128)S(1)}) all-reduce(f32[1,32,32]{2,1,0:T(8,128)S(1)} %convolution_bitcast_fusion.1, f32[1,32,32]{2,1,0:T(8,128)S(1)} %convolution_bitcast_fusion), channel_id=1, replica_groups=mesh['dp'=32,'tensor'=16] {'tensor'}, use_global_device_ids=true, to_apply=%region_3.0 | all-reduce | flops 2048 | bytes 16384 | tf_op jit(solution)/shard_map/psum | solution.py:27
  225.5 0.6 multiply_reduce_fusion
  226.8 1.3 dynamic-slice
  228.1 0.7 dynamic-update-slice
  228.8 60.1 %all-reduce = f32[32]{0:T(128)S(1)} all-reduce(f32[32]{0:T(128)S(1)} %dynamic-update-slice), channel_id=1, replica_groups=mesh['dp'=32,'tensor'=16] {'dp'}, use_global_device_ids=true, to_apply=%add | all-reduce | flops 32 | bytes 256
  288.9 0.0 all-reduce.5.cloned.1.call-done
  288.9 3.4 %mul.6 = f32[384,1024]{1,0:T(8,128)} multiply(f32[384,1024]{1,0:T(8,128)} %get-tuple-element.7, f32[384,1024]{1,0:T(8,128)} %get-tuple-element.8) | non-fusion elementwise | flops 393216 | bytes 4718592 | tf_op jit(solution)/shard_map/mul | solution.py:32
  292.3 1.9 copy.5
  294.2 0.2 bitcast_reduce_fusion
  294.4 0.7 divide_bitcast_fusion
  (1 shorter events, 0.0 us)
Async XLA Ops:
  6.5 152.2 %copy-start = (bf16[384,1792]{1,0:T(8,128)(2,1)S(1)}, bf16[384,1792]{1,0:T(8,128)(2,1)}, u32[]{:S(2)}) copy-start(bf16[384,1792]{1,0:T(8,128)(2,1)} %param.4) | copy-start | bytes 4128772
  6.5 79.3 %all-gather.5.cloned.1.call-start = ((), (), s32[]{:S(2)}) async-start(), calls=%async_computation.1 | async-start | bytes 1081344 | tf_op jit(solution)/shard_map/all_gather | solution.py:26
  7.3 151.5 %all-gather.3.cloned.1.call-start = ((), (), s32[]{:S(2)}) async-start(), calls=%async_computation | async-start | bytes 3784704 | tf_op jit(solution)/shard_map/all_gather | solution.py:25
  8.0 280.9 %all-reduce.5.cloned.1.call-start = ((), (), s32[]{:S(2)}) async-start(), calls=%async_computation.2 | async-start | bytes 6291456 | tf_op jit(solution)/shard_map/psum | solution.py:30
  163.6 0.8 copy-start.2
  163.6 0.9 copy-start.1
Sparse Core Ops, SparseCore 0:
  9.5 76.3 all-gather.4
  88.0 70.7 all-gather.2
  163.8 122.8 all-reduce.4
where the time goes:
time: 302 us
  waiting for transfers between devices  149 us (49%)
  blocking collectives  121 us (40%)
  between operations  13.8 us (5%)
  matrix products  8.22 us (3%)
  other arithmetic  4.88 us (2%)
  local copies, waits for them, and re-layouts  4.65 us (2%)
    all_gather x1, waiting for transfers between devices, on_device(): lax.all_gather(query_right, 'dp', axis=0, tiled=True)  77.8 us
    all_gather x1, waiting for transfers between devices, on_device(): lax.all_gather(query_left, 'dp', axis=0, tiled=True)  69.7 us
    psum x1, blocking collectives, on_device(): lax.psum((own_gram(query_left), own_gram(query_right)), 'tensor')  60.8 us
    unnamed x1, blocking collectives  60.1 us
    dot_general x2, matrix products, contract(): jnp.einsum('tf,kf->tk', rows_here, factors, preferred_element_type=jnp.fl...  7.97 us
  transfers between devices with their start and end apart: 3, of which 2 were waited for; matrix products, arithmetic and copies ran while one was open for 2% of the time, Pallas kernels for 0%

commit v1 on v0

v1 whole, which is shorter than its diff:
```python
import jax
import jax.numpy as jnp
from jax import lax
from jax.experimental import pallas as pl
from jax.experimental.pallas import tpu as pltpu
from jax.sharding import Mesh
from jax.sharding import PartitionSpec as P

R = 32
GROUP = 128

epsilon = 1e-06

NT = (((1,), (1,)), ((), ()))


def _project(q_ref, own_ref, other_ref, out_ref):
    n_own, n_other = own_ref.shape[0], other_ref.shape[0]
    q = q_ref[...]
    out_ref[:, :n_own] = lax.dot_general(q, own_ref[...], NT, preferred_element_type=jnp.float32)
    out_ref[:, n_own : n_own + n_other] = lax.dot_general(
        q, other_ref[...], NT, preferred_element_type=jnp.float32
    )
    out_ref[:, n_own + n_other :] = lax.dot_general(q, q, NT, preferred_element_type=jnp.float32)


def project(q, own, other):
    rows, k = q.shape
    tokens = own.shape[0] + other.shape[0]
    width = tokens + GROUP
    whole = lambda a: pl.BlockSpec(a.shape, lambda i: (0, 0))
    return pl.pallas_call(
        _project,
        grid=(rows // GROUP,),
        in_specs=[pl.BlockSpec((GROUP, k), lambda i: (i, 0)), whole(own), whole(other)],
        out_specs=pl.BlockSpec((GROUP, width), lambda i: (i, 0)),
        out_shape=jax.ShapeDtypeStruct((rows, width), jnp.float32),
        compiler_params=pltpu.CompilerParams(vmem_limit_bytes=40 * 2**20),
        cost_estimate=pl.CostEstimate(
            flops=2 * rows * k * width,
            bytes_accessed=2 * k * (rows + tokens) + 4 * rows * width,
            transcendentals=0,
        ),
    )(q, own, other)


def _finish(slot_ref, left_ref, right_ref, out_ref):
    left, right = left_ref[0], right_ref[0]
    for s in range(1, left_ref.shape[0]):
        left = left + left_ref[s]
        right = right + right_ref[s]
    both = jnp.sum(left * right, axis=0, keepdims=True)
    tokens = out_ref.shape[1]
    lanes = lax.broadcasted_iota(jnp.int32, (1, GROUP), 1)
    mine = lanes // R == slot_ref[0]
    square = jnp.sum(jnp.where(mine, both[:, tokens:], 0.0), axis=1, keepdims=True)
    out_ref[...] = both[:, :tokens] / jnp.sqrt(square + epsilon)


def finish(slot, left, right):
    tokens = left.shape[2] - GROUP
    return pl.pallas_call(
        _finish,
        in_specs=[
            pl.BlockSpec(memory_space=pltpu.SMEM),
            pl.BlockSpec(memory_space=pltpu.VMEM),
            pl.BlockSpec(memory_space=pltpu.VMEM),
        ],
        out_specs=pl.BlockSpec(memory_space=pltpu.VMEM),
        out_shape=jax.ShapeDtypeStruct((1, tokens), jnp.float32),
        compiler_params=pltpu.CompilerParams(vmem_limit_bytes=40 * 2**20),
        cost_estimate=pl.CostEstimate(
            flops=4 * left.size, bytes_accessed=8 * left.size, transcendentals=0
        ),
    )(slot, left, right)


def on_device(hidden_acts, out_grads, query_left, query_right):
    planes = lax.axis_size("z")
    owners = lax.axis_size(("x", "y"))
    tokens = hidden_acts.shape[0]
    swap = [(0, 1), (1, 0)]
    hidden_other = lax.ppermute(hidden_acts, "c", swap)
    grads_other = lax.ppermute(out_grads, "c", swap)
    left_rows = lax.all_gather(query_left, "z", axis=0, tiled=True)
    right_rows = lax.all_gather(query_right, "z", axis=0, tiled=True)

    def owned(rows, own, other):
        terms = project(rows, own, other)
        terms = terms.reshape(owners, terms.shape[0] // owners, terms.shape[1])
        return lax.all_to_all(terms, ("x", "y"), split_axis=0, concat_axis=0, tiled=True)

    right = owned(right_rows, out_grads, grads_other)
    left = owned(left_rows, hidden_acts, hidden_other)
    slot = lax.rem(lax.axis_index(("x", "y")), GROUP // R).astype(jnp.int32).reshape(1)
    scores = finish(slot, left, right)

    core = lax.axis_index("c")
    halves = scores.reshape(2, tokens)
    by_core = jnp.where(core == 0, halves, halves[::-1])
    sent = jnp.broadcast_to(by_core[:, None, :], (2, owners, tokens)).reshape(2 * owners, 1, tokens)
    got = lax.all_to_all(sent, ("c", "x", "y"), split_axis=0, concat_axis=0, tiled=True)
    return got.reshape(2, planes, tokens).transpose(1, 0, 2).reshape(2 * planes, tokens)


def solution(mesh):
    devices = mesh.devices
    planes = devices.shape[0] // 2
    owners = devices.shape[1]
    side = int(round(owners**0.5))
    grid = Mesh(devices.reshape(planes, 2, side, side), ("z", "c", "x", "y"))
    placed = P(("z", "c"), ("x", "y"))
    return jax.shard_map(
        on_device,
        mesh=grid,
        in_specs=(placed,) * 4,
        out_specs=P(None, ("z", "c")),
        check_vma=False,
    )
```

time: 302 us -> 143 us (0.47)
  waiting for transfers between devices: 149 us -> 33 us
  blocking collectives: 121 us -> 49 us
  starting transfers between devices: 0.08 us -> 30.7 us
  matrix products: 8.22 us -> 0 us
  Pallas kernels: 0 us -> 7.55 us
  other arithmetic: 4.88 us -> 0.03 us
  local copies, waits for them, and re-layouts: 4.65 us -> 8.29 us
    all_gather x2 -> x1, waiting for transfers between devices: 148 us -> 12.4 us  [on_device(): left_rows = lax.all_gather(query_left, 'z', axis=0, tiled=True)]
    psum x1 -> x0, blocking collectives: 60.8 us -> none  [on_device(): lax.psum((own_gram(query_left), own_gram(query_right)), 'tensor')]
    unnamed x1 -> x0, blocking collectives: 60.1 us -> none
    all_gather x0 -> x1, blocking collectives: none -> 27.8 us  [on_device(): right_rows = lax.all_gather(query_right, 'z', axis=0, tiled=True)]
    all_to_all x0 -> x1, blocking collectives: none -> 21.2 us  [on_device(): lax.all_to_all(sent, ('c', 'x', 'y'), split_axis=0, concat_axis=0, tiled=...]
    all_to_all x0 -> x2, waiting for transfers between devices: none -> 17.2 us  [owned(): lax.all_to_all(terms, ('x', 'y'), split_axis=0, concat_axis=0, tiled=True)]
    ppermute x0 -> x2, starting transfers between devices: none -> 16.3 us  [the longest x1 8.79 us: on_device(): grads_other = lax.ppermute(out_grads, 'c', swap)]
    all_to_all x0 -> x2, starting transfers between devices: none -> 14.4 us  [owned(): lax.all_to_all(terms, ('x', 'y'), split_axis=0, concat_axis=0, tiled=True)]
  transfers between devices with their start and end apart: 3 -> 5, of which waited for: 2 -> 3; matrix products, arithmetic and copies ran while one was open for 2% -> 0% of each run, Pallas kernels for 0% -> 4%
where the time goes in v1:
time: 143 us; the launch traced here: 142 us
  blocking collectives  49 us (34%)
  waiting for transfers between devices  33 us (23%)
  starting transfers between devices  30.7 us (21%)
  between operations  13.5 us (9%)
  local copies, waits for them, and re-layouts  8.29 us (6%)
  Pallas kernels  7.55 us (5%)
    all_gather x1, blocking collectives, on_device(): right_rows = lax.all_gather(query_right, 'z', axis=0, tiled=True)  27.8 us
    all_to_all x1, blocking collectives, on_device(): lax.all_to_all(sent, ('c', 'x', 'y'), split_axis=0, concat_axis=0, tiled=...  21.2 us
    all_to_all x2, waiting for transfers between devices, owned(): lax.all_to_all(terms, ('x', 'y'), split_axis=0, concat_axis=0, tiled=True)  17.2 us
    all_to_all x2, starting transfers between devices, owned(): lax.all_to_all(terms, ('x', 'y'), split_axis=0, concat_axis=0, tiled=True)  14.4 us
    all_gather x1, waiting for transfers between devices, on_device(): left_rows = lax.all_gather(query_left, 'z', axis=0, tiled=True)  12.4 us
    ppermute x1, starting transfers between devices, on_device(): grads_other = lax.ppermute(out_grads, 'c', swap)  8.79 us
    ppermute x1, starting transfers between devices, on_device(): hidden_other = lax.ppermute(hidden_acts, 'c', swap)  7.53 us
    unnamed x15, local copies, waits for them, and re-layouts  7.44 us
  transfers between devices with their start and end apart: 5, of which 3 were waited for; matrix products, arithmetic and copies ran while one was open for 0% of the time, Pallas kernels for 4%

profile of v1, /device:TPU:1, one launch (start us, length us, event | category | flops | bytes accessed | tf_op | source)
XLA Modules:
  0.0 142.1 jit_solution(3050780732476647920)
XLA Ops:
  6.5 0.0 all-gather.2.cloned.1.call-start
  6.5 0.7 all-gather.2.cloned.1.call-update
  7.3 8.8 %collective-permute-start.1 = (bf16[384,512]{1,0:T(8,128)(2,1)}, bf16[384,512]{1,0:T(8,128)(2,1)S(1)}, u32[]{:S(2)}, u32[]{:S(2)}) collective-permute-start(bf16[384,512]{1,0:T(8,128)(2,1)} %own_ref.3), channel_id=1, source_target_pairs={{0,16},{16,0},{1,17},{17,1},{2,18},{18,2},{3,19},{19,3},{4,20},{20... | collective-permute-start | bytes 1179656 | tf_op jit(solution)/shard_map/ppermute | solution.py:84
  16.1 27.8 %all_gather.7.q_ref = bf16[512,512]{1,0:T(8,128)(2,1)S(1)} all-gather(bf16[32,512]{1,0:T(8,128)(2,1)} %param.7), channel_id=1, replica_groups=mesh['z'=16,'c'=2,'x'=4,'y'=4] {'z'}, dimensions={0}, use_global_device_ids=true | all-gather | bytes 557056 | tf_op jit(solution)/shard_map/all_gather | solution.py:86
  43.9 0.0 collective-permute-done.1.other_ref
  43.9 0.0 copy-start.6
  43.9 1.0 copy-done.6
  44.9 1.7 %shard_map.47 = f32[512,896]{1,0:T(8,128)S(1)} custom-call(bf16[512,512]{1,0:T(8,128)(2,1)S(1)} %all_gather.7.q_ref, bf16[384,512]{1,0:T(8,128)(2,1)S(1)} %copy-done.6, bf16[384,512]{1,0:T(8,128)(2,1)S(1)} %collective-permute-done.1.other_ref), custom_call_target="tpu_custom_call" | custom-call | flops 469762048 | bytes 3145728 | tf_op jit(solution)/shard_map/pallas_call | solution.py:32
  46.5 0.0 copy-start.1
  46.5 1.3 copy-done.1
  47.8 0.0 copy-start.3
  47.8 7.3 %all-to-all-start.1 = ((f32[16,32,896]{2,1,0:T(8,128)}), f32[16,32,896]{2,1,0:T(8,128)S(1)}, u32[]{:S(2)}, u32[]{:S(2)}) async-start(f32[16,32,896]{2,1,0:T(8,128)} %bitcast.7), calls=%async_computation.1 | async-start | bytes 3670016 | tf_op jit(solution)/shard_map/all_to_all | solution.py:91
  55.1 0.0 copy-done.3
  55.1 7.5 %collective-permute-start = (bf16[384,1792]{1,0:T(8,128)(2,1)S(1)}, bf16[384,1792]{1,0:T(8,128)(2,1)S(1)}, u32[]{:S(2)}, u32[]{:S(2)}) collective-permute-start(bf16[384,1792]{1,0:T(8,128)(2,1)S(1)} %copy-done.3), channel_id=1, source_target_pairs={{0,16},{16,0},{1,17},{17,1},{2,18},{18,2},{3,19},{19,3},{4,20},{20... | collective-permute-start | bytes 4128776 | tf_op jit(solution)/shard_map/ppermute | solution.py:83
  62.6 2.7 %collective-permute-done.other_ref = bf16[384,1792]{1,0:T(8,128)(2,1)S(1)} collective-permute-done((bf16[384,1792]{1,0:T(8,128)(2,1)S(1)}, bf16[384,1792]{1,0:T(8,128)(2,1)S(1)}, u32[]{:S(2)}, u32[]{:S(2)}) %collective-permute-start) | collective-permute-done | bytes 1376288 | tf_op jit(solution)/shard_map/ppermute | solution.py:83
  65.3 0.0 copy-start.4
  65.3 1.1 copy-done.4
  66.4 12.4 %all-gather.2.cloned.1.call-done.q_ref = bf16[512,1792]{1,0:T(8,128)(2,1)} async-done(((bf16[32,1792]{1,0:T(8,128)(2,1)}), bf16[512,1792]{1,0:T(8,128)(2,1)}) %all-gather.2.cloned.1.call-update) | async-done | bytes 1835024 | tf_op jit(solution)/shard_map/all_gather | solution.py:85
  78.8 0.0 copy-start.2
  78.8 1.5 %copy-done.2 = bf16[512,1792]{1,0:T(8,128)(2,1)S(1)} copy-done((bf16[512,1792]{1,0:T(8,128)(2,1)S(1)}, bf16[512,1792]{1,0:T(8,128)(2,1)}, u32[]{:S(2)}) %copy-start.2) | copy-done | bytes 1835032
  80.3 0.0 copy-start.5
  80.3 1.3 copy-done.5
  81.6 4.2 %shard_map.46 = f32[512,896]{1,0:T(8,128)S(1)} custom-call(bf16[512,1792]{1,0:T(8,128)(2,1)S(1)} %copy-done.2, bf16[384,1792]{1,0:T(8,128)(2,1)S(1)} %copy-done.3, bf16[384,1792]{1,0:T(8,128)(2,1)S(1)} %copy-done.5), custom_call_target="tpu_custom_call" | custom-call | flops 1644167168 | bytes 6422528 | tf_op jit(solution)/shard_map/pallas_call | solution.py:32
  85.8 0.0 copy-start
  85.8 1.2 copy-done
  87.1 0.0 all-to-all-done.1.right_ref
  87.1 7.1 %all-to-all-start = ((f32[16,32,896]{2,1,0:T(8,128)}), f32[16,32,896]{2,1,0:T(8,128)}, u32[]{:S(2)}, u32[]{:S(2)}) async-start(f32[16,32,896]{2,1,0:T(8,128)} %bitcast.6), calls=%async_computation | async-start | bytes 3670016 | tf_op jit(solution)/shard_map/all_to_all | solution.py:91
  94.2 17.2 %all-to-all-done.left_ref = f32[16,32,896]{2,1,0:T(8,128)} async-done(((f32[16,32,896]{2,1,0:T(8,128)}), f32[16,32,896]{2,1,0:T(8,128)}, u32[]{:S(2)}, u32[]{:S(2)}) %all-to-all-start) | async-done | bytes 1835040 | tf_op jit(solution)/shard_map/all_to_all | solution.py:91
  111.4 1.7 %shard_map.48 = f32[1,768]{1,0:T(1,128)S(1)} custom-call(s32[1]{0:T(128)} %bitcast.slot_ref, f32[16,32,896]{2,1,0:T(8,128)} %all-to-all-done.left_ref, f32[16,32,896]{2,1,0:T(8,128)S(1)} %all-to-all-done.1.right_ref), custom_call_target="tpu_custom_call" | custom-call | flops 1835008 | bytes 3670016 | tf_op jit(solution)/shard_map/pallas_call | solution.py:62
  113.2 0.1 rev.3
  113.4 21.2 %all_to_all.15 = f32[32,1,384]{2,1,0:T(1,128)S(1)} all-to-all(f32[32,1,384]{2,1,0:T(1,128)S(1)} %reshape.26), channel_id=1, replica_groups=mesh['z'=16,'c'=2,'x'=4,'y'=4] {'c','x','y'}, dimensions={0} | all-to-all | bytes 98304 | tf_op jit(solution)/shard_map/all_to_all | solution.py:102
  134.6 0.7 reshape.28
  (7 shorter events, 0.1 us)
Async XLA Ops:
  6.5 72.3 %all-gather.2.cloned.1.call-start = ((), (), s32[]{:S(2)}) async-start(), calls=%async_computation.3 | async-start | bytes 1949696 | tf_op jit(solution)/shard_map/all_gather | solution.py:85
  7.3 36.6 %collective-permute-start.1 = (bf16[384,512]{1,0:T(8,128)(2,1)}, bf16[384,512]{1,0:T(8,128)(2,1)S(1)}, u32[]{:S(2)}, u32[]{:S(2)}) collective-permute-start(bf16[384,512]{1,0:T(8,128)(2,1)} %own_ref.3), channel_id=1, source_target_pairs={{0,16},{16,0},{1,17},{17,1},{2,18},{18,2},{3,19},{19,3},{4,20},{20... | collective-permute-start | bytes 1179656 | tf_op jit(solution)/shard_map/ppermute | solution.py:84
  43.9 1.0 copy-start.6
  46.5 1.3 copy-start.1
  47.8 7.3 %copy-start.3 = (bf16[384,1792]{1,0:T(8,128)(2,1)S(1)}, bf16[384,1792]{1,0:T(8,128)(2,1)}, u32[]{:S(2)}) copy-start(bf16[384,1792]{1,0:T(8,128)(2,1)} %own_ref.2) | copy-start | bytes 4128772
  47.8 39.3 %all-to-all-start.1 = ((f32[16,32,896]{2,1,0:T(8,128)}), f32[16,32,896]{2,1,0:T(8,128)S(1)}, u32[]{:S(2)}, u32[]{:S(2)}) async-start(f32[16,32,896]{2,1,0:T(8,128)} %bitcast.7), calls=%async_computation.1 | async-start | bytes 3670016 | tf_op jit(solution)/shard_map/all_to_all | solution.py:91
  55.1 10.3 %collective-permute-start = (bf16[384,1792]{1,0:T(8,128)(2,1)S(1)}, bf16[384,1792]{1,0:T(8,128)(2,1)S(1)}, u32[]{:S(2)}, u32[]{:S(2)}) collective-permute-start(bf16[384,1792]{1,0:T(8,128)(2,1)S(1)} %copy-done.3), channel_id=1, source_target_pairs={{0,16},{16,0},{1,17},{17,1},{2,18},{18,2},{3,19},{19,3},{4,20},{20... | collective-permute-start | bytes 4128776 | tf_op jit(solution)/shard_map/ppermute | solution.py:83
  65.3 1.1 copy-start.4
  78.8 1.5 %copy-start.2 = (bf16[512,1792]{1,0:T(8,128)(2,1)S(1)}, bf16[512,1792]{1,0:T(8,128)(2,1)}, u32[]{:S(2)}) copy-start(bf16[512,1792]{1,0:T(8,128)(2,1)} %all-gather.2.cloned.1.call-done.q_ref) | copy-start | bytes 5505028
  80.3 1.3 copy-start.5
  85.8 1.3 copy-start
  87.1 24.4 %all-to-all-start = ((f32[16,32,896]{2,1,0:T(8,128)}), f32[16,32,896]{2,1,0:T(8,128)}, u32[]{:S(2)}, u32[]{:S(2)}) async-start(f32[16,32,896]{2,1,0:T(8,128)} %bitcast.6), calls=%async_computation | async-start | bytes 3670016 | tf_op jit(solution)/shard_map/all_to_all | solution.py:91
Sparse Core Ops, SparseCore 0:
  9.4 69.3 all-gather.1

commit v2 on v1

v2 whole, which is shorter than its diff:
```python
import jax
import jax.numpy as jnp
from jax import lax
from jax.experimental import pallas as pl
from jax.experimental.pallas import tpu as pltpu
from jax.sharding import Mesh
from jax.sharding import PartitionSpec as P

R = 32
GROUP = 128
TOP = 2.0**15
POWERS = (64, 32, 16, 8, 4, 2, 1)

epsilon = 1e-06

NT = (((1,), (1,)), ((), ()))
VMEM = pl.BlockSpec(memory_space=pltpu.VMEM)
SMEM = pl.BlockSpec(memory_space=pltpu.SMEM)


def params():
    return pltpu.CompilerParams(vmem_limit_bytes=40 * 2**20)


def dot(a, b):
    return lax.dot_general(a, b, NT, preferred_element_type=jnp.float32)


def pack(left, right):
    rows, wide = left.shape
    narrow = right.shape[1]

    def scaled(x):
        x = x.astype(jnp.float32)
        largest = jnp.maximum(jnp.max(jnp.abs(x), axis=1, keepdims=True), 2.0**-100)
        scale, exponent = jnp.ones_like(largest), jnp.zeros_like(largest)
        for p in POWERS:
            more = largest * (scale * 2.0**p) < TOP
            scale = jnp.where(more, scale * 2.0**p, scale)
            exponent = jnp.where(more, exponent + p, exponent)
        return x * scale, exponent

    def body(left_ref, right_ref, out):
        left_rows, left_exponent = scaled(left_ref[...])
        right_rows, right_exponent = scaled(right_ref[...])
        out[:, :wide] = left_rows.astype(out.dtype)
        out[:, wide : wide + narrow] = right_rows.astype(out.dtype)
        lanes = lax.broadcasted_iota(jnp.int32, (rows, GROUP), 1)
        out[:, wide + narrow :] = jnp.where(lanes == 0, left_exponent, right_exponent).astype(out.dtype)

    return pl.pallas_call(
        body,
        in_specs=[VMEM] * 2,
        out_specs=VMEM,
        out_shape=jax.ShapeDtypeStruct((rows, wide + narrow + GROUP), left.dtype),
        compiler_params=params(),
    )(left, right)


def unscaled(rows, exponent):
    factor = jnp.ones_like(exponent)
    for p in POWERS:
        more = exponent >= p
        factor = jnp.where(more, factor * 2.0**-p, factor)
        exponent = jnp.where(more, exponent - p, exponent)
    return (rows.astype(jnp.float32) * factor).astype(rows.dtype)


def project(queries, hidden, hidden_other, grads, grads_other):
    rows = queries.shape[0]
    own, wide = hidden.shape
    narrow = grads.shape[1]
    width = 4 * own + GROUP

    def body(q_ref, h, ho, g, go, out):
        exponents = q_ref[:, wide + narrow :].astype(jnp.float32)
        left = unscaled(q_ref[:, :wide], exponents[:, 0:1])
        right = unscaled(q_ref[:, wide : wide + narrow], exponents[:, 1:2])
        out[:, :own] = dot(left, h[...])
        out[:, own : 2 * own] = dot(left, ho[...])
        out[:, 2 * own : 3 * own] = dot(right, g[...])
        out[:, 3 * own : 4 * own] = dot(right, go[...])
        query = lax.broadcasted_iota(jnp.int32, (GROUP, GROUP), 0) // R
        block = lax.broadcasted_iota(jnp.int32, (GROUP, GROUP), 1) // R
        next_right = jnp.concatenate([right[GROUP - R :], right[: GROUP - R]], axis=0)
        out[:, 4 * own :] = jnp.where(query == block, dot(left, left), dot(right, next_right))

    whole = lambda a: pl.BlockSpec(a.shape, lambda i: (0, 0))
    tokens = (hidden, hidden_other, grads, grads_other)
    return pl.pallas_call(
        body,
        grid=(rows // GROUP,),
        in_specs=[pl.BlockSpec((GROUP, queries.shape[1]), lambda i: (i, 0))]
        + [whole(a) for a in tokens],
        out_specs=pl.BlockSpec((GROUP, width), lambda i: (i, 0)),
        out_shape=jax.ShapeDtypeStruct((rows, width), jnp.float32),
        compiler_params=params(),
        cost_estimate=pl.CostEstimate(
            flops=rows * width * queries.shape[1],
            bytes_accessed=2 * (2 * own + rows) * queries.shape[1] + 4 * rows * width,
            transcendentals=0,
        ),
    )(queries, *tokens)


def finish(slot, terms):
    own = (terms.shape[2] - GROUP) // 4

    def body(slot_ref, terms_ref, out):
        total = terms_ref[0]
        for s in range(1, terms_ref.shape[0]):
            total = total + terms_ref[s]
        both = jnp.sum(total[:, : 2 * own] * total[:, 2 * own : 4 * own], axis=0, keepdims=True)
        gram = total[:, 4 * own :]
        gram = gram * pltpu.roll(gram, GROUP - R, 1)
        lanes = lax.broadcasted_iota(jnp.int32, (1, GROUP), 1)
        mine = lanes // R == slot_ref[0]
        square = jnp.sum(jnp.where(mine, gram, 0.0), axis=(0, 1), keepdims=True)
        out[...] = both / jnp.sqrt(square + epsilon)

    return pl.pallas_call(
        body,
        in_specs=[SMEM, VMEM],
        out_specs=VMEM,
        out_shape=jax.ShapeDtypeStruct((1, 2 * own), jnp.float32),
        compiler_params=params(),
    )(slot, terms)


def on_device(hidden_acts, out_grads, query_left, query_right):
    planes = lax.axis_size("z")
    owners = lax.axis_size(("x", "y"))
    tokens = hidden_acts.shape[0]
    swap = [(0, 1), (1, 0)]
    hidden_other = lax.ppermute(hidden_acts, "c", swap)
    grads_other = lax.ppermute(out_grads, "c", swap)

    sent = pack(query_left, query_right).astype(jnp.float16)
    queries = lax.all_gather(sent, "z", axis=0, tiled=True).astype(query_left.dtype)
    terms = project(queries, hidden_acts, hidden_other, out_grads, grads_other)
    terms = terms.reshape(owners, terms.shape[0] // owners, terms.shape[1])
    terms = lax.all_to_all(terms, ("x", "y"), split_axis=0, concat_axis=0, tiled=True)
    slot = lax.rem(lax.axis_index(("x", "y")), GROUP // R).astype(jnp.int32).reshape(1)
    scores = finish(slot, terms)

    halves = scores.reshape(2, tokens)
    by_core = jnp.where(lax.axis_index("c") == 0, halves, halves[::-1])
    sent = jnp.broadcast_to(by_core[:, None, :], (2, owners, tokens)).reshape(2 * owners, 1, tokens)
    got = lax.all_to_all(sent, ("c", "x", "y"), split_axis=0, concat_axis=0, tiled=True)
    return got.reshape(2, planes, tokens).transpose(1, 0, 2).reshape(2 * planes, tokens)


def solution(mesh):
    devices = mesh.devices
    planes = devices.shape[0] // 2
    owners = devices.shape[1]
    side = int(round(owners**0.5))
    grid = Mesh(devices.reshape(planes, 2, side, side), ("z", "c", "x", "y"))
    placed = P(("z", "c"), ("x", "y"))
    return jax.shard_map(
        on_device,
        mesh=grid,
        in_specs=(placed,) * 4,
        out_specs=P(None, ("z", "c")),
        check_vma=False,
    )
```

time: 143 us -> 132 us (0.923)
  blocking collectives: 49 us -> 65.1 us
  between operations: 13.5 us -> 0.15 us
  starting transfers between devices: 30.7 us -> 17.5 us
  waiting for transfers between devices: 33 us -> 37.1 us
  local copies, waits for them, and re-layouts: 8.29 us -> 5.27 us
  Pallas kernels: 7.55 us -> 5.69 us
    all_to_all x2 -> x1, waiting for transfers between devices: 17.2 us -> 37.1 us  [on_device(): lax.all_to_all(terms, ('x', 'y'), split_axis=0, concat_axis=0, tiled=True)]
    all_gather x1, blocking collectives: 27.8 us -> 41.6 us  [on_device(): lax.all_gather(sent, 'z', axis=0, tiled=True).astype(query_left.dtype)]
    all_gather x1 -> x0, waiting for transfers between devices: 12.4 us -> none  [on_device(): left_rows = lax.all_gather(query_left, 'z', axis=0, tiled=True)]
    all_to_all x2 -> x1, starting transfers between devices: 14.4 us -> 6.76 us  [on_device(): lax.all_to_all(terms, ('x', 'y'), split_axis=0, concat_axis=0, tiled=True)]
    ppermute x1, starting transfers between devices: 8.79 us -> 1.92 us  [on_device(): grads_other = lax.ppermute(out_grads, 'c', swap)]
    unnamed x15 -> x11, local copies, waits for them, and re-layouts: 7.44 us -> 4.43 us
    ppermute x1, waiting for transfers between devices: 2.73 us -> 0.01 us  [on_device(): hidden_other = lax.ppermute(hidden_acts, 'c', swap)]
    all_to_all x1, blocking collectives: 21.2 us -> 23.6 us  [on_device(): lax.all_to_all(sent, ('c', 'x', 'y'), split_axis=0, concat_axis=0, tiled=...]
  transfers between devices with their start and end apart: 5 -> 3, of which waited for: 3 -> 1; matrix products, arithmetic and copies ran while one was open for 0% -> 0% of each run, Pallas kernels for 4% -> 0%
where the time goes in v2:
time: 132 us; the launch traced here: 131 us
  blocking collectives  65.1 us (49%)
  waiting for transfers between devices  37.1 us (28%)
  starting transfers between devices  17.5 us (13%)
  Pallas kernels  5.69 us (4%)
  local copies, waits for them, and re-layouts  5.27 us (4%)
    all_gather x1, blocking collectives, on_device(): lax.all_gather(sent, 'z', axis=0, tiled=True).astype(query_left.dtype)  41.6 us
    all_to_all x1, waiting for transfers between devices, on_device(): lax.all_to_all(terms, ('x', 'y'), split_axis=0, concat_axis=0, tiled=True)  37.1 us
    all_to_all x1, blocking collectives, on_device(): lax.all_to_all(sent, ('c', 'x', 'y'), split_axis=0, concat_axis=0, tiled=...  23.6 us
    ppermute x1, starting transfers between devices, on_device(): hidden_other = lax.ppermute(hidden_acts, 'c', swap)  8.78 us
    all_to_all x1, starting transfers between devices, on_device(): lax.all_to_all(terms, ('x', 'y'), split_axis=0, concat_axis=0, tiled=True)  6.76 us
    pallas_call x1, Pallas kernels, project(): pl.pallas_call(body, grid=(rows // GROUP,), in_specs=[pl.BlockSpec((GROUP...  5.22 us
    unnamed x11, local copies, waits for them, and re-layouts  4.43 us
  transfers between devices with their start and end apart: 3, of which 1 were waited for; matrix products, arithmetic and copies ran while one was open for 0% of the time, Pallas kernels for 0%

profile of v2, /device:TPU:1, one launch (start us, length us, event | category | flops | bytes accessed | tf_op | source)
XLA Modules:
  0.0 131.2 jit_solution(15486936508825204745)
XLA Ops:
  0.0 8.8 %collective-permute-start = (bf16[384,1792]{1,0:T(8,128)(2,1)}, bf16[384,1792]{1,0:T(8,128)(2,1)S(1)}, u32[]{:S(2)}, u32[]{:S(2)}) collective-permute-start(bf16[384,1792]{1,0:T(8,128)(2,1)} %h.1), channel_id=1, source_target_pairs={{0,16},{16,0},{1,17},{17,1},{2,18},{18,2},{3,19},{19,3},{4,20},{20... | collective-permute-start | bytes 4128776 | tf_op jit(solution)/shard_map/ppermute | solution.py:135
  8.8 1.9 %collective-permute-start.1 = (bf16[384,512]{1,0:T(8,128)(2,1)}, bf16[384,512]{1,0:T(8,128)(2,1)S(1)}, u32[]{:S(2)}, u32[]{:S(2)}) collective-permute-start(bf16[384,512]{1,0:T(8,128)(2,1)} %g.1), channel_id=1, source_target_pairs={{0,16},{16,0},{1,17},{17,1},{2,18},{18,2},{3,19},{19,3},{4,20},{20... | collective-permute-start | bytes 1179656 | tf_op jit(solution)/shard_map/ppermute | solution.py:136
  10.7 0.0 copy-start.3
  10.7 0.9 copy-done.3
  11.6 0.0 copy-start.4
  11.6 0.8 copy-done.4
  12.4 0.2 shard_map.46
  12.6 41.6 %all-gather.1 = f16[512,2432]{1,0:T(8,128)(2,1)S(1)} all-gather(f16[32,2432]{1,0:T(8,128)(2,1)S(1)} %convert_element_type.6), channel_id=1, replica_groups=mesh['z'=16,'c'=2,'x'=4,'y'=4] {'z'}, dimensions={0}, use_global_device_ids=true | all-gather | bytes 2646016 | tf_op jit(solution)/shard_map/all_gather | solution.py:139
  54.2 0.0 copy-start.1
  54.2 0.0 copy-start.2
  54.2 0.3 convert_element_type.7.q_ref
  54.5 0.0 collective-permute-done.1.go
  54.5 0.0 collective-permute-done.ho
  54.5 1.0 copy-done.1
  55.5 0.1 copy-done.2
  55.6 5.2 %shard_map.47 = f32[512,1664]{1,0:T(8,128)S(1)} custom-call(bf16[512,2432]{1,0:T(8,128)(2,1)S(1)} %convert_element_type.7.q_ref, bf16[384,1792]{1,0:T(8,128)(2,1)S(1)} %copy-done.1, bf16[384,1792]{1,0:T(8,128)(2,1)S(1)} %collective-permute-done.ho, bf16[384,512]{1,0:T(8,128)(2,1)S(1)} %copy-done.2, bf16[384,512]{1,0:T(8,128)(2,1)S(1)} %collective-permute-done.1.go), custom_call_target="tpu_custom_call" | custom-call | flops 2071986176 | bytes 9633792 | tf_op jit(solution)/shard_map/pallas_call | solution.py:90
  60.8 0.0 copy-start
  60.8 1.7 %copy-done = f32[512,1664]{1,0:T(8,128)} copy-done((f32[512,1664]{1,0:T(8,128)}, f32[512,1664]{1,0:T(8,128)S(1)}, u32[]{:S(2)}) %copy-start) | copy-done | bytes 3407896
  62.5 6.8 %all-to-all-start = ((f32[16,32,1664]{2,1,0:T(8,128)}), f32[16,32,1664]{2,1,0:T(8,128)S(1)}, u32[]{:S(2)}, u32[]{:S(2)}) async-start(f32[16,32,1664]{2,1,0:T(8,128)} %bitcast.5), calls=%async_computation | async-start | bytes 6815744 | tf_op jit(solution)/shard_map/all_to_all | solution.py:142
  69.3 37.1 %all-to-all-done.terms_ref = f32[16,32,1664]{2,1,0:T(8,128)S(1)} async-done(((f32[16,32,1664]{2,1,0:T(8,128)}), f32[16,32,1664]{2,1,0:T(8,128)S(1)}, u32[]{:S(2)}, u32[]{:S(2)}) %all-to-all-start) | async-done | bytes 3407904 | tf_op jit(solution)/shard_map/all_to_all | solution.py:142
  106.4 0.3 shard_map.48
  106.7 0.1 rev.3
  106.9 23.6 %all_to_all.10 = f32[32,1,384]{2,1,0:T(1,128)S(1)} all-to-all(f32[32,1,384]{2,1,0:T(1,128)S(1)} %reshape.22), channel_id=1, replica_groups=mesh['z'=16,'c'=2,'x'=4,'y'=4] {'c','x','y'}, dimensions={0} | all-to-all | bytes 98304 | tf_op jit(solution)/shard_map/all_to_all | solution.py:149
  130.5 0.7 reshape.24
  (8 shorter events, 0.1 us)
Async XLA Ops:
  0.0 54.5 %collective-permute-start = (bf16[384,1792]{1,0:T(8,128)(2,1)}, bf16[384,1792]{1,0:T(8,128)(2,1)S(1)}, u32[]{:S(2)}, u32[]{:S(2)}) collective-permute-start(bf16[384,1792]{1,0:T(8,128)(2,1)} %h.1), channel_id=1, source_target_pairs={{0,16},{16,0},{1,17},{17,1},{2,18},{18,2},{3,19},{19,3},{4,20},{20... | collective-permute-start | bytes 4128776 | tf_op jit(solution)/shard_map/ppermute | solution.py:135
  8.8 45.7 %collective-permute-start.1 = (bf16[384,512]{1,0:T(8,128)(2,1)}, bf16[384,512]{1,0:T(8,128)(2,1)S(1)}, u32[]{:S(2)}, u32[]{:S(2)}) collective-permute-start(bf16[384,512]{1,0:T(8,128)(2,1)} %g.1), channel_id=1, source_target_pairs={{0,16},{16,0},{1,17},{17,1},{2,18},{18,2},{3,19},{19,3},{4,20},{20... | collective-permute-start | bytes 1179656 | tf_op jit(solution)/shard_map/ppermute | solution.py:136
  10.7 0.9 copy-start.3
  11.6 0.8 copy-start.4
  54.2 1.3 %copy-start.1 = (bf16[384,1792]{1,0:T(8,128)(2,1)S(1)}, bf16[384,1792]{1,0:T(8,128)(2,1)}, u32[]{:S(2)}) copy-start(bf16[384,1792]{1,0:T(8,128)(2,1)} %h.1) | copy-start | bytes 4128772
  54.2 1.4 %copy-start.2 = (bf16[384,512]{1,0:T(8,128)(2,1)S(1)}, bf16[384,512]{1,0:T(8,128)(2,1)}, u32[]{:S(2)}) copy-start(bf16[384,512]{1,0:T(8,128)(2,1)} %g.1) | copy-start | bytes 1179652
  60.8 1.7 %copy-start = (f32[512,1664]{1,0:T(8,128)}, f32[512,1664]{1,0:T(8,128)S(1)}, u32[]{:S(2)}) copy-start(f32[512,1664]{1,0:T(8,128)S(1)} %shard_map.47) | copy-start | bytes 10223620
  62.5 43.9 %all-to-all-start = ((f32[16,32,1664]{2,1,0:T(8,128)}), f32[16,32,1664]{2,1,0:T(8,128)S(1)}, u32[]{:S(2)}, u32[]{:S(2)}) async-start(f32[16,32,1664]{2,1,0:T(8,128)} %bitcast.5), calls=%async_computation | async-start | bytes 6815744 | tf_op jit(solution)/shard_map/all_to_all | solution.py:142

commit v3 on v2

v3 whole, which is shorter than its diff:
```python
import jax
import jax.numpy as jnp
from jax import lax
from jax.experimental import pallas as pl
from jax.experimental.pallas import tpu as pltpu
from jax.sharding import Mesh
from jax.sharding import PartitionSpec as P

R = 32
GROUP = 128
CLASSES = 2
TOP = 2.0**15
POWERS = (64, 32, 16, 8, 4, 2, 1)
WEIGHTS = (20, 0.01)

epsilon = 1e-06

NT = (((1,), (1,)), ((), ()))
VMEM = pl.BlockSpec(memory_space=pltpu.VMEM)
SMEM = pl.BlockSpec(memory_space=pltpu.SMEM)


def params():
    return pltpu.CompilerParams(vmem_limit_bytes=16 * 2**20)


def dot(a, b):
    return lax.dot_general(a, b, NT, preferred_element_type=jnp.float32)


def pack(left, right):
    rows, wide = left.shape
    narrow = right.shape[1]

    def scaled(x):
        x = x.astype(jnp.float32)
        largest = jnp.maximum(jnp.max(jnp.abs(x), axis=1, keepdims=True), 2.0**-100)
        scale, exponent = jnp.ones_like(largest), jnp.zeros_like(largest)
        for p in POWERS:
            more = largest * (scale * 2.0**p) < TOP
            scale = jnp.where(more, scale * 2.0**p, scale)
            exponent = jnp.where(more, exponent + p, exponent)
        return x * scale, exponent

    def body(left_ref, right_ref, out):
        left_rows, left_exponent = scaled(left_ref[...])
        right_rows, right_exponent = scaled(right_ref[...])
        out[:, :wide] = left_rows.astype(out.dtype)
        out[:, wide : wide + narrow] = right_rows.astype(out.dtype)
        lanes = lax.broadcasted_iota(jnp.int32, (rows, GROUP), 1)
        out[:, wide + narrow :] = jnp.where(lanes == 0, left_exponent, right_exponent).astype(out.dtype)

    return pl.pallas_call(
        body,
        in_specs=[VMEM] * 2,
        out_specs=VMEM,
        out_shape=jax.ShapeDtypeStruct((rows, wide + narrow + GROUP), left.dtype),
        compiler_params=params(),
    )(left, right)


def unscaled(rows, exponent):
    factor = jnp.ones_like(exponent)
    for p in POWERS:
        more = exponent >= p
        factor = jnp.where(more, factor * 2.0**-p, factor)
        exponent = jnp.where(more, exponent - p, exponent)
    return (rows.astype(jnp.float32) * factor).astype(rows.dtype)


def project(weight, pieces, hidden, hidden_other, grads, grads_other):
    rows = sum(p.shape[0] for p in pieces)
    packed = pieces[0].shape[1]
    own, wide = hidden.shape
    narrow = grads.shape[1]
    width = 4 * own + GROUP

    def body(*refs):
        q_refs, (h, ho, g, go, out) = refs[: len(pieces)], refs[len(pieces) :]
        blocks = [(q, at) for q in q_refs for at in range(0, q.shape[0], GROUP)]
        query = lax.broadcasted_iota(jnp.int32, (GROUP, GROUP), 0) // R
        block = lax.broadcasted_iota(jnp.int32, (GROUP, GROUP), 1) // R
        for i, (q_ref, at) in enumerate(blocks):
            here, there = slice(at, at + GROUP), slice(i * GROUP, (i + 1) * GROUP)
            exponents = q_ref[here, wide + narrow :].astype(jnp.float32)
            left = unscaled(q_ref[here, :wide], exponents[:, 0:1])
            right = unscaled(q_ref[here, wide : wide + narrow], exponents[:, 1:2])
            out[there, :own] = dot(left, h[...])
            out[there, own : 2 * own] = dot(left, ho[...])
            out[there, 2 * own : 3 * own] = dot(right, g[...])
            out[there, 3 * own : 4 * own] = dot(right, go[...])
            next_right = jnp.concatenate([right[GROUP - R :], right[: GROUP - R]], axis=0)
            out[there, 4 * own :] = jnp.where(query == block, dot(left, left), dot(right, next_right))

    return pl.pallas_call(
        body,
        in_specs=[VMEM] * (len(pieces) + 4),
        out_specs=VMEM,
        out_shape=jax.ShapeDtypeStruct((rows, width), jnp.float32),
        compiler_params=params(),
        cost_estimate=pl.CostEstimate(
            flops=int(weight * rows * width * packed),
            bytes_accessed=int(weight * 2 * rows * packed),
            transcendentals=0,
        ),
    )(*pieces, hidden, hidden_other, grads, grads_other)


def finish(place, parts):
    owners = parts[0].shape[0]
    own = (parts[0].shape[2] - GROUP) // 4

    def body(place_ref, *refs):
        out = refs[-1]
        core, parity, slot = place_ref[0], place_ref[1], place_ref[2]
        lanes = lax.broadcasted_iota(jnp.int32, (1, GROUP), 1)
        at = lax.broadcasted_iota(jnp.int32, (CLASSES, own + GROUP), 0)
        mine = jnp.zeros((CLASSES, own + GROUP), jnp.float32)
        theirs = mine
        for k, ref in enumerate(refs[:-1]):
            total = ref[0]
            for s in range(1, owners):
                total = total + ref[s]
            both = jnp.sum(total[:, : 2 * own] * total[:, 2 * own : 4 * own], axis=0, keepdims=True)
            gram = total[:, 4 * own :]
            gram = gram * pltpu.roll(gram, GROUP - R, 1)
            square = jnp.sum(jnp.where(lanes // R == slot, gram, 0.0), axis=(0, 1), keepdims=True)
            square = jnp.broadcast_to(square, (1, GROUP))
            row = at == lax.rem(parity + k, CLASSES)
            mine = jnp.where(row, jnp.concatenate([both[:, :own], square], 1), mine)
            theirs = jnp.where(row, jnp.concatenate([both[:, own:], square], 1), theirs)
        first = jnp.where(core == 0, mine, theirs)
        second = jnp.where(core == 0, theirs, mine)
        out[:owners] = jnp.broadcast_to(first[None], (owners, *first.shape))
        out[owners:] = jnp.broadcast_to(second[None], (owners, *second.shape))

    return pl.pallas_call(
        body,
        in_specs=[SMEM] + [VMEM] * len(parts),
        out_specs=VMEM,
        out_shape=jax.ShapeDtypeStruct((2 * owners, CLASSES, own + GROUP), jnp.float32),
        compiler_params=params(),
    )(place, *parts)


def scores_of(got, shares):
    own = got.shape[2] - GROUP
    queries = got.shape[0] // 2 // shares

    def body(got_ref, out):
        for core in range(2):
            for a in range(queries):
                first = (core * queries + a) * shares
                total = got_ref[first]
                for b in range(1, shares):
                    total = total + got_ref[first + b]
                values = total[:, :own] / jnp.sqrt(total[:, own : own + 1] + epsilon)
                for g in range(CLASSES):
                    row = 2 * (CLASSES * a + g) + core
                    out[row : row + 1, :] = values[g : g + 1]

    return pl.pallas_call(
        body,
        in_specs=[VMEM],
        out_specs=VMEM,
        out_shape=jax.ShapeDtypeStruct((2 * CLASSES * queries, own), jnp.float32),
        compiler_params=params(),
    )(got)


def on_device(hidden_acts, out_grads, query_left, query_right):
    planes = lax.axis_size(("zh", "zp"))
    owners = lax.axis_size(("x", "y"))

    def from_plane(block, ahead):
        pairs = [((z + ahead) % planes, z) for z in range(planes)]
        return lax.ppermute(block, ("zh", "zp"), pairs)

    swap = [(0, 1), (1, 0)]
    hidden_other = lax.ppermute(hidden_acts, "c", swap)
    grads_other = lax.ppermute(out_grads, "c", swap)
    tokens = (hidden_acts, hidden_other, out_grads, grads_other)

    sent = pack(query_left, query_right).astype(jnp.float16)
    here = lax.all_gather(sent, "zh", axis=0, tiled=True).astype(query_left.dtype)
    half = here.shape[0] // 2
    there = (from_plane(here[:half], 1), from_plane(here[half:], -1))

    def owned(terms):
        terms = terms.reshape(owners, terms.shape[0] // owners, terms.shape[1])
        return lax.all_to_all(terms, ("x", "y"), split_axis=0, concat_axis=0, tiled=True)

    first_terms = project(WEIGHTS[0], (here,), *tokens)
    first = owned(first_terms)
    there, _ = lax.optimization_barrier((there, first_terms))
    second_terms, first = lax.optimization_barrier((project(WEIGHTS[1], there, *tokens), first))
    second = owned(second_terms)

    share = here.shape[0] // owners
    shares = R // share
    place = jnp.stack(
        [
            lax.axis_index("c"),
            lax.axis_index("zp"),
            lax.rem(lax.axis_index(("x", "y")) // shares, GROUP // R),
        ]
    ).astype(jnp.int32)
    sums = finish(place, (first, second))
    got = lax.all_to_all(sums, ("c", "x", "y"), split_axis=0, concat_axis=0, tiled=True)
    return scores_of(got, shares)


def solution(mesh):
    devices = mesh.devices
    planes = devices.shape[0] // 2
    owners = devices.shape[1]
    side = int(round(owners**0.5))
    shape = (planes // CLASSES, CLASSES, 2, side, side)
    grid = Mesh(devices.reshape(shape), ("zh", "zp", "c", "x", "y"))
    placed = P(("zh", "zp", "c"), ("x", "y"))
    return jax.shard_map(
        on_device,
        mesh=grid,
        in_specs=(placed,) * 4,
        out_specs=P(None, ("zh", "zp", "c")),
        check_vma=False,
    )
```

time: 132 us -> 125 us (0.947)
  starting transfers between devices: 17.5 us -> 31 us
  waiting for transfers between devices: 37.1 us -> 24.8 us
  blocking collectives: 65.1 us -> 54.7 us
  Pallas kernels: 5.69 us -> 7.84 us
    all_to_all x1 -> x2, waiting for transfers between devices: 37.1 us -> 15.9 us  [owned(): lax.all_to_all(terms, ('x', 'y'), split_axis=0, concat_axis=0, tiled=True)]
    ppermute x0 -> x2, waiting for transfers between devices: none -> 8.91 us  [from_plane(): return lax.ppermute(block, ('zh', 'zp'), pairs)]
    all_gather x1, blocking collectives: 41.6 us -> 33.3 us  [on_device(): lax.all_gather(sent, 'zh', axis=0, tiled=True).astype(query_left.dtype)]
    all_to_all x1 -> x2, starting transfers between devices: 6.76 us -> 13.7 us  [owned(): lax.all_to_all(terms, ('x', 'y'), split_axis=0, concat_axis=0, tiled=True)]
    ppermute x0 -> x2, starting transfers between devices: none -> 6.62 us  [from_plane(): return lax.ppermute(block, ('zh', 'zp'), pairs)]
    all_to_all x1, blocking collectives: 23.6 us -> 21.4 us  [on_device(): lax.all_to_all(sums, ('c', 'x', 'y'), split_axis=0, concat_axis=0, tiled=...]
    pallas_call x2 -> x4, Pallas kernels: 5.53 us -> 7.68 us  [the longest x2 6.16 us: project(): pl.pallas_call(body, in_specs=[VMEM] * (len(pieces) + 4), out_specs=VMEM,...]
    unnamed x11 -> x20, local copies, waits for them, and re-layouts: 4.43 us -> 5.57 us
  transfers between devices with their start and end apart: 3 -> 6, of which waited for: 1 -> 3; matrix products, arithmetic and copies ran while one was open for 0% -> 0% of each run, Pallas kernels for 0% -> 3%
where the time goes in v3:
time: 125 us; the launch traced here: 124 us
  blocking collectives  54.7 us (44%)
  starting transfers between devices  31 us (25%)
  waiting for transfers between devices  24.8 us (20%)
  Pallas kernels  7.84 us (6%)
  local copies, waits for them, and re-layouts  5.66 us (5%)
    all_gather x1, blocking collectives, on_device(): lax.all_gather(sent, 'zh', axis=0, tiled=True).astype(query_left.dtype)  33.3 us
    all_to_all x1, blocking collectives, on_device(): lax.all_to_all(sums, ('c', 'x', 'y'), split_axis=0, concat_axis=0, tiled=...  21.4 us
    all_to_all x2, waiting for transfers between devices, owned(): lax.all_to_all(terms, ('x', 'y'), split_axis=0, concat_axis=0, tiled=True)  15.9 us
    all_to_all x2, starting transfers between devices, owned(): lax.all_to_all(terms, ('x', 'y'), split_axis=0, concat_axis=0, tiled=True)  13.7 us
    ppermute x2, waiting for transfers between devices, from_plane(): return lax.ppermute(block, ('zh', 'zp'), pairs)  8.91 us
    ppermute x1, starting transfers between devices, on_device(): hidden_other = lax.ppermute(hidden_acts, 'c', swap)  8.78 us
    ppermute x2, starting transfers between devices, from_plane(): return lax.ppermute(block, ('zh', 'zp'), pairs)  6.62 us
    pallas_call x2, Pallas kernels, project(): pl.pallas_call(body, in_specs=[VMEM] * (len(pieces) + 4), out_specs=VMEM,...  6.16 us
  transfers between devices with their start and end apart: 6, of which 3 were waited for; matrix products, arithmetic and copies ran while one was open for 0% of the time, Pallas kernels for 3%

profile of v3, /device:TPU:1, one launch (start us, length us, event | category | flops | bytes accessed | tf_op | source)
XLA Modules:
  0.0 124.4 jit_solution(1801722192721231714)
XLA Ops:
  0.0 8.8 %collective-permute-start.2 = (bf16[384,1792]{1,0:T(8,128)(2,1)}, bf16[384,1792]{1,0:T(8,128)(2,1)S(1)}, u32[]{:S(2)}, u32[]{:S(2)}) collective-permute-start(bf16[384,1792]{1,0:T(8,128)(2,1)} %refs_2_.1), channel_id=1, source_target_pairs={{0,16},{16,0},{1,17},{17,1},{2,18},{18,2},{3,19},{19,3},{4,20},{20... | collective-permute-start | bytes 4128776 | tf_op jit(solution)/shard_map/ppermute | solution.py:180
  8.8 1.9 %collective-permute-start.3 = (bf16[384,512]{1,0:T(8,128)(2,1)}, bf16[384,512]{1,0:T(8,128)(2,1)S(1)}, u32[]{:S(2)}, u32[]{:S(2)}) collective-permute-start(bf16[384,512]{1,0:T(8,128)(2,1)} %refs_4_.1), channel_id=1, source_target_pairs={{0,16},{16,0},{1,17},{17,1},{2,18},{18,2},{3,19},{19,3},{4,20},{20... | collective-permute-start | bytes 1179656 | tf_op jit(solution)/shard_map/ppermute | solution.py:181
  10.7 0.0 copy-start.8
  10.7 0.9 copy-done.8
  11.6 0.8 copy-done.9
  12.4 0.2 shard_map.46
  12.6 33.3 %all-gather.1 = f16[256,2432]{1,0:T(8,128)(2,1)S(1)} all-gather(f16[32,2432]{1,0:T(8,128)(2,1)S(1)} %convert_element_type.6), channel_id=1, replica_groups=mesh['zh'=8,'zp'=2,'c'=2,'x'=4,'y'=4] {'zh'}, dimensions={0}, use_global_device_ids=true | all-gather | bytes 1400832 | tf_op jit(solution)/shard_map/all_gather | solution.py:185
  45.9 0.1 convert_element_type.7.refs_0_
  46.0 0.0 collective-permute-done.3.refs_4_.refs_5_
  46.0 0.0 copy-start.6
  46.0 0.0 collective-permute-done.2.refs_2_.refs_3_
  46.1 1.3 %copy-done.1 = bf16[384,1792]{1,0:T(8,128)(2,1)S(1)} copy-done((bf16[384,1792]{1,0:T(8,128)(2,1)S(1)}, bf16[384,1792]{1,0:T(8,128)(2,1)}, u32[]{:S(2)}) %copy-start.1) | copy-done | bytes 1376280
  47.4 0.1 copy-done.5
  47.4 2.5 %shard_map.47 = f32[256,1664]{1,0:T(8,128)S(1)} custom-call(bf16[256,2432]{1,0:T(8,128)(2,1)S(1)} %convert_element_type.7.refs_0_, bf16[384,1792]{1,0:T(8,128)(2,1)S(1)} %copy-done.1, bf16[384,1792]{1,0:T(8,128)(2,1)S(1)} %collective-permute-done.2.refs_2_.refs_3_, bf16[384,512]{1,0:T(8,128)(2,1)S(1)} %copy-done.5, ...), custom_call_target="tpu_custom_call" | custom-call | flops 20719861760 | bytes 24903680 | tf_op jit(solution)/shard_map/pallas_call | solution.py:95
  49.9 1.2 copy-done
  51.1 7.3 %all-to-all-start = ((f32[16,16,1664]{2,1,0:T(8,128)}), f32[16,16,1664]{2,1,0:T(8,128)S(1)}, u32[]{:S(2)}, u32[]{:S(2)}) async-start(f32[16,16,1664]{2,1,0:T(8,128)} %bitcast.5), calls=%async_computation | async-start | bytes 3407872 | tf_op jit(solution)/shard_map/all_to_all | solution.py:191
  58.5 0.0 copy-start.2
  58.5 0.1 fusion
  58.6 2.2 %collective-permute-start.1 = (bf16[128,2432]{1,0:T(8,128)(2,1)S(1)}, bf16[128,2432]{1,0:T(8,128)(2,1)S(1)}, u32[]{:S(2)}, u32[]{:S(2)}) collective-permute-start(bf16[128,2432]{1,0:T(8,128)(2,1)S(1)} %get-tuple-element.13), channel_id=1, source_target_pairs={{480,0},{0,32},{32,64},{64,96},{96,128},{128,160},{160,192},{192,2... | collective-permute-start | bytes 1867784 | tf_op jit(solution)/shard_map/ppermute | solution.py:177
  60.7 4.5 %collective-permute-start = (bf16[128,2432]{1,0:T(8,128)(2,1)S(1)}, bf16[128,2432]{1,0:T(8,128)(2,1)S(1)}, u32[]{:S(2)}, u32[]{:S(2)}) collective-permute-start(bf16[128,2432]{1,0:T(8,128)(2,1)S(1)} %get-tuple-element.14), channel_id=1, source_target_pairs={{32,0},{64,32},{96,64},{128,96},{160,128},{192,160},{224,192},{256... | collective-permute-start | bytes 1867784 | tf_op jit(solution)/shard_map/ppermute | solution.py:177
  65.2 6.4 %collective-permute-done.1.refs_1_ = bf16[128,2432]{1,0:T(8,128)(2,1)S(1)} collective-permute-done((bf16[128,2432]{1,0:T(8,128)(2,1)S(1)}, bf16[128,2432]{1,0:T(8,128)(2,1)S(1)}, u32[]{:S(2)}, u32[]{:S(2)}) %collective-permute-start.1) | collective-permute-done | bytes 622624 | tf_op jit(solution)/shard_map/ppermute | solution.py:177
  71.6 2.5 %collective-permute-done.refs_0_ = bf16[128,2432]{1,0:T(8,128)(2,1)S(1)} collective-permute-done((bf16[128,2432]{1,0:T(8,128)(2,1)S(1)}, bf16[128,2432]{1,0:T(8,128)(2,1)S(1)}, u32[]{:S(2)}, u32[]{:S(2)}) %collective-permute-start) | collective-permute-done | bytes 622624 | tf_op jit(solution)/shard_map/ppermute | solution.py:177
  74.1 0.0 copy-done.2
  74.1 1.3 %copy-done.4 = bf16[384,1792]{1,0:T(8,128)(2,1)S(1)} copy-done((bf16[384,1792]{1,0:T(8,128)(2,1)S(1)}, bf16[384,1792]{1,0:T(8,128)(2,1)}, u32[]{:S(2)}) %copy-start.4) | copy-done | bytes 1376280
  75.5 3.7 %shard_map.48 = f32[256,1664]{1,0:T(8,128)} custom-call(bf16[128,2432]{1,0:T(8,128)(2,1)S(1)} %collective-permute-done.refs_0_, bf16[128,2432]{1,0:T(8,128)(2,1)S(1)} %collective-permute-done.1.refs_1_, bf16[384,1792]{1,0:T(8,128)(2,1)S(1)} %copy-done.2, bf16[384,1792]{1,0:T(8,128)(2,1)S(1)} %copy-done.4, bf16[384,512]{1,0:T(8,128)(2,1)S(1)} %copy-done.5, ...), custom_call_target="tpu_custom_call" | custom-call | flops 10359930 | bytes 12451 | tf_op jit(solution)/shard_map/pallas_call | solution.py:95
  79.2 0.0 all-to-all-done.refs_0_
  79.2 6.4 %all-to-all-start.1 = ((f32[16,16,1664]{2,1,0:T(8,128)}), f32[16,16,1664]{2,1,0:T(8,128)S(1)}, u32[]{:S(2)}, u32[]{:S(2)}) async-start(f32[16,16,1664]{2,1,0:T(8,128)} %bitcast.4), calls=%async_computation.1 | async-start | bytes 3407872 | tf_op jit(solution)/shard_map/all_to_all | solution.py:191
  85.6 0.1 pad_add_fusion.place_ref
  85.7 15.9 %all-to-all-done.1.refs_1_ = f32[16,16,1664]{2,1,0:T(8,128)S(1)} async-done(((f32[16,16,1664]{2,1,0:T(8,128)}), f32[16,16,1664]{2,1,0:T(8,128)S(1)}, u32[]{:S(2)}, u32[]{:S(2)}) %all-to-all-start.1) | async-done | bytes 1703968 | tf_op jit(solution)/shard_map/all_to_all | solution.py:191
  101.5 0.8 shard_map.49
  102.3 21.4 %all_to_all.15.got_ref = f32[32,2,512]{2,1,0:T(2,128)S(1)} all-to-all(f32[32,2,512]{2,1,0:T(2,128)S(1)} %shard_map.49), channel_id=1, replica_groups=mesh['zh'=8,'zp'=2,'c'=2,'x'=4,'y'=4] {'c','x','y'}, dimensions={0} | all-to-all | bytes 262144 | tf_op jit(solution)/shard_map/all_to_all | solution.py:209
  123.7 0.7 shard_map.50
  (11 shorter events, 0.0 us)
Async XLA Ops:
  0.0 46.1 %collective-permute-start.2 = (bf16[384,1792]{1,0:T(8,128)(2,1)}, bf16[384,1792]{1,0:T(8,128)(2,1)S(1)}, u32[]{:S(2)}, u32[]{:S(2)}) collective-permute-start(bf16[384,1792]{1,0:T(8,128)(2,1)} %refs_2_.1), channel_id=1, source_target_pairs={{0,16},{16,0},{1,17},{17,1},{2,18},{18,2},{3,19},{19,3},{4,20},{20... | collective-permute-start | bytes 4128776 | tf_op jit(solution)/shard_map/ppermute | solution.py:180
  8.8 37.2 %collective-permute-start.3 = (bf16[384,512]{1,0:T(8,128)(2,1)}, bf16[384,512]{1,0:T(8,128)(2,1)S(1)}, u32[]{:S(2)}, u32[]{:S(2)}) collective-permute-start(bf16[384,512]{1,0:T(8,128)(2,1)} %refs_4_.1), channel_id=1, source_target_pairs={{0,16},{16,0},{1,17},{17,1},{2,18},{18,2},{3,19},{19,3},{4,20},{20... | collective-permute-start | bytes 1179656 | tf_op jit(solution)/shard_map/ppermute | solution.py:181
  10.7 0.9 copy-start.8
  11.6 0.8 copy-start.9
  45.9 1.5 %copy-start.1 = (bf16[384,1792]{1,0:T(8,128)(2,1)S(1)}, bf16[384,1792]{1,0:T(8,128)(2,1)}, u32[]{:S(2)}) copy-start(bf16[384,1792]{1,0:T(8,128)(2,1)} %refs_2_.1) | copy-start | bytes 4128772
  45.9 1.6 %copy-start.5 = (bf16[384,512]{1,0:T(8,128)(2,1)S(1)}, bf16[384,512]{1,0:T(8,128)(2,1)}, u32[]{:S(2)}) copy-start(bf16[384,512]{1,0:T(8,128)(2,1)} %refs_4_.1) | copy-start | bytes 1179652
  46.0 3.9 %copy-start.6 = (bf16[384,512]{1,0:T(8,128)(2,1)}, bf16[384,512]{1,0:T(8,128)(2,1)S(1)}, u32[]{:S(2)}) copy-start(bf16[384,512]{1,0:T(8,128)(2,1)S(1)} %collective-permute-done.3.refs_4_.refs_5_) | copy-start | bytes 1179652
  47.4 2.5 %copy-start.3 = (bf16[384,1792]{1,0:T(8,128)(2,1)}, bf16[384,1792]{1,0:T(8,128)(2,1)S(1)}, u32[]{:S(2)}) copy-start(bf16[384,1792]{1,0:T(8,128)(2,1)S(1)} %collective-permute-done.2.refs_2_.refs_3_) | copy-start | bytes 4128772
  49.9 1.2 copy-start
  51.1 28.0 %all-to-all-start = ((f32[16,16,1664]{2,1,0:T(8,128)}), f32[16,16,1664]{2,1,0:T(8,128)S(1)}, u32[]{:S(2)}, u32[]{:S(2)}) async-start(f32[16,16,1664]{2,1,0:T(8,128)} %bitcast.5), calls=%async_computation | async-start | bytes 3407872 | tf_op jit(solution)/shard_map/all_to_all | solution.py:191
  58.5 15.7 %copy-start.2 = (bf16[384,1792]{1,0:T(8,128)(2,1)S(1)}, bf16[384,1792]{1,0:T(8,128)(2,1)}, u32[]{:S(2)}) copy-start(bf16[384,1792]{1,0:T(8,128)(2,1)} %refs_2_.1) | copy-start | bytes 4128772
  58.5 15.7 %copy-start.7 = (bf16[384,512]{1,0:T(8,128)(2,1)S(1)}, bf16[384,512]{1,0:T(8,128)(2,1)}, u32[]{:S(2)}) copy-start(bf16[384,512]{1,0:T(8,128)(2,1)} %copy-done.6) | copy-start | bytes 1179652
  58.6 13.1 %collective-permute-start.1 = (bf16[128,2432]{1,0:T(8,128)(2,1)S(1)}, bf16[128,2432]{1,0:T(8,128)(2,1)S(1)}, u32[]{:S(2)}, u32[]{:S(2)}) collective-permute-start(bf16[128,2432]{1,0:T(8,128)(2,1)S(1)} %get-tuple-element.13), channel_id=1, source_target_pairs={{480,0},{0,32},{32,64},{64,96},{96,128},{128,160},{160,192},{192,2... | collective-permute-start | bytes 1867784 | tf_op jit(solution)/shard_map/ppermute | solution.py:177
  60.7 13.4 %collective-permute-start = (bf16[128,2432]{1,0:T(8,128)(2,1)S(1)}, bf16[128,2432]{1,0:T(8,128)(2,1)S(1)}, u32[]{:S(2)}, u32[]{:S(2)}) collective-permute-start(bf16[128,2432]{1,0:T(8,128)(2,1)S(1)} %get-tuple-element.14), channel_id=1, source_target_pairs={{32,0},{64,32},{96,64},{128,96},{160,128},{192,160},{224,192},{256... | collective-permute-start | bytes 1867784 | tf_op jit(solution)/shard_map/ppermute | solution.py:177
  74.1 1.3 %copy-start.4 = (bf16[384,1792]{1,0:T(8,128)(2,1)S(1)}, bf16[384,1792]{1,0:T(8,128)(2,1)}, u32[]{:S(2)}) copy-start(bf16[384,1792]{1,0:T(8,128)(2,1)} %copy-done.3) | copy-start | bytes 4128772
  79.2 22.3 %all-to-all-start.1 = ((f32[16,16,1664]{2,1,0:T(8,128)}), f32[16,16,1664]{2,1,0:T(8,128)S(1)}, u32[]{:S(2)}, u32[]{:S(2)}) async-start(f32[16,16,1664]{2,1,0:T(8,128)} %bitcast.4), calls=%async_computation.1 | async-start | bytes 3407872 | tf_op jit(solution)/shard_map/all_to_all | solution.py:191

commit v4 on v3

--- a/solution.py
+++ b/solution.py
@@ -68,42 +68,49 @@
     return (rows.astype(jnp.float32) * factor).astype(rows.dtype)
 
 
-def project(weight, pieces, hidden, hidden_other, grads, grads_other):
+def project(weight, wide, pieces, mine, theirs):
     rows = sum(p.shape[0] for p in pieces)
     packed = pieces[0].shape[1]
-    own, wide = hidden.shape
-    narrow = grads.shape[1]
+    own, both = mine.shape
     width = 4 * own + GROUP
 
     def body(*refs):
-        q_refs, (h, ho, g, go, out) = refs[: len(pieces)], refs[len(pieces) :]
-        blocks = [(q, at) for q in q_refs for at in range(0, q.shape[0], GROUP)]
+        q_refs, (mine_ref, theirs_ref, out, left, right) = refs[: len(pieces)], refs[len(pieces) :]
+        at = 0
+        for q_ref in q_refs:
+            here = slice(at, at + q_ref.shape[0])
+            exponents = q_ref[:, both:].astype(jnp.float32)
+            left[here] = unscaled(q_ref[:, :wide], exponents[:, 0:1])
+            right[here] = unscaled(q_ref[:, wide:both], exponents[:, 1:2])
+            at += q_ref.shape[0]
+        out[:, :own] = dot(left[...], mine_ref[:, :wide])
+        out[:, own : 2 * own] = dot(left[...], theirs_ref[:, :wide])
+        out[:, 2 * own : 3 * own] = dot(right[...], mine_ref[:, wide:])
+        out[:, 3 * own : 4 * own] = dot(right[...], theirs_ref[:, wide:])
         query = lax.broadcasted_iota(jnp.int32, (GROUP, GROUP), 0) // R
         block = lax.broadcasted_iota(jnp.int32, (GROUP, GROUP), 1) // R
-        for i, (q_ref, at) in enumerate(blocks):
-            here, there = slice(at, at + GROUP), slice(i * GROUP, (i + 1) * GROUP)
-            exponents = q_ref[here, wide + narrow :].astype(jnp.float32)
-            left = unscaled(q_ref[here, :wide], exponents[:, 0:1])
-            right = unscaled(q_ref[here, wide : wide + narrow], exponents[:, 1:2])
-            out[there, :own] = dot(left, h[...])
-            out[there, own : 2 * own] = dot(left, ho[...])
-            out[there, 2 * own : 3 * own] = dot(right, g[...])
-            out[there, 3 * own : 4 * own] = dot(right, go[...])
-            next_right = jnp.concatenate([right[GROUP - R :], right[: GROUP - R]], axis=0)
-            out[there, 4 * own :] = jnp.where(query == block, dot(left, left), dot(right, next_right))
-
-    return pl.pallas_call(
-        body,
-        in_specs=[VMEM] * (len(pieces) + 4),
+        for at in range(0, rows, GROUP):
+            here = slice(at, at + GROUP)
+            x, y = left[here], right[here]
+            next_y = jnp.concatenate([y[GROUP - R :], y[: GROUP - R]], axis=0)
+            out[here, 4 * own :] = jnp.where(query == block, dot(x, x), dot(y, next_y))
+
+    return pl.pallas_call(
+        body,
+        in_specs=[VMEM] * (len(pieces) + 2),
         out_specs=VMEM,
         out_shape=jax.ShapeDtypeStruct((rows, width), jnp.float32),
+        scratch_shapes=[
+            pltpu.VMEM((rows, wide), mine.dtype),
+            pltpu.VMEM((rows, both - wide), mine.dtype),
+        ],
         compiler_params=params(),
         cost_estimate=pl.CostEstimate(
             flops=int(weight * rows * width * packed),
             bytes_accessed=int(weight * 2 * rows * packed),
             transcendentals=0,
         ),
-    )(*pieces, hidden, hidden_other, grads, grads_other)
+    )(*pieces, mine, theirs)
 
 
 def finish(place, parts):
@@ -176,27 +183,27 @@
         pairs = [((z + ahead) % planes, z) for z in range(planes)]
         return lax.ppermute(block, ("zh", "zp"), pairs)
 
-    swap = [(0, 1), (1, 0)]
-    hidden_other = lax.ppermute(hidden_acts, "c", swap)
-    grads_other = lax.ppermute(out_grads, "c", swap)
-    tokens = (hidden_acts, hidden_other, out_grads, grads_other)
+    mine = jnp.concatenate([hidden_acts, out_grads], axis=1)
+    tokens = (mine, lax.ppermute(mine, "c", [(0, 1), (1, 0)]))
+    wide = hidden_acts.shape[1]
 
     sent = pack(query_left, query_right).astype(jnp.float16)
-    here = lax.all_gather(sent, "zh", axis=0, tiled=True).astype(query_left.dtype)
+    here = lax.all_gather(sent, "zh", axis=0, tiled=True)
     half = here.shape[0] // 2
-    there = (from_plane(here[:half], 1), from_plane(here[half:], -1))
+    here = (here[:half].astype(query_left.dtype), here[half:].astype(query_left.dtype))
+    there = (from_plane(here[0], 1), from_plane(here[1], -1))
 
     def owned(terms):
         terms = terms.reshape(owners, terms.shape[0] // owners, terms.shape[1])
         return lax.all_to_all(terms, ("x", "y"), split_axis=0, concat_axis=0, tiled=True)
 
-    first_terms = project(WEIGHTS[0], (here,), *tokens)
+    first_terms = project(WEIGHTS[0], wide, here, *tokens)
     first = owned(first_terms)
     there, _ = lax.optimization_barrier((there, first_terms))
-    second_terms, first = lax.optimization_barrier((project(WEIGHTS[1], there, *tokens), first))
+    second_terms, first = lax.optimization_barrier((project(WEIGHTS[1], wide, there, *tokens), first))
     second = owned(second_terms)
 
-    share = here.shape[0] // owners
+    share = 2 * half // owners
     shares = R // share
     place = jnp.stack(
         [

time: 125 us -> 119 us (0.952)
  starting transfers between devices: 31 us -> 28 us
  local copies, waits for them, and re-layouts: 5.66 us -> 4.19 us
  Pallas kernels: 7.84 us -> 6.52 us
    ppermute x2 -> x1, starting transfers between devices: 10.7 us -> 8.78 us  [on_device(): tokens = (mine, lax.ppermute(mine, 'c', [(0, 1), (1, 0)]))]
    unnamed x20 -> x17, local copies, waits for them, and re-layouts: 5.57 us -> 4.16 us
    pallas_call x2, Pallas kernels: 6.16 us -> 4.83 us  [project(): pl.pallas_call(body, in_specs=[VMEM] * (len(pieces) + 2), out_specs=VMEM,...]
  transfers between devices with their start and end apart: 6 -> 5, of which waited for: 3 -> 3; matrix products, arithmetic and copies ran while one was open for 0% -> 0% of each run, Pallas kernels for 3% -> 3%
where the time goes in v4:
time: 119 us; the launch traced here: 118 us
  blocking collectives  55.3 us (46%)
  starting transfers between devices  28 us (24%)
  waiting for transfers between devices  24 us (20%)
  Pallas kernels  6.52 us (5%)
  local copies, waits for them, and re-layouts  4.19 us (4%)
    all_gather x1, blocking collectives, on_device(): here = lax.all_gather(sent, 'zh', axis=0, tiled=True)  34.3 us
    all_to_all x1, blocking collectives, on_device(): lax.all_to_all(sums, ('c', 'x', 'y'), split_axis=0, concat_axis=0, tiled=...  21 us
    all_to_all x2, waiting for transfers between devices, owned(): lax.all_to_all(terms, ('x', 'y'), split_axis=0, concat_axis=0, tiled=True)  16.2 us
    all_to_all x2, starting transfers between devices, owned(): lax.all_to_all(terms, ('x', 'y'), split_axis=0, concat_axis=0, tiled=True)  12.7 us
    ppermute x1, starting transfers between devices, on_device(): tokens = (mine, lax.ppermute(mine, 'c', [(0, 1), (1, 0)]))  8.78 us
    ppermute x2, waiting for transfers between devices, from_plane(): return lax.ppermute(block, ('zh', 'zp'), pairs)  7.82 us
    ppermute x2, starting transfers between devices, from_plane(): return lax.ppermute(block, ('zh', 'zp'), pairs)  6.49 us
    pallas_call x2, Pallas kernels, project(): pl.pallas_call(body, in_specs=[VMEM] * (len(pieces) + 2), out_specs=VMEM,...  4.83 us
  transfers between devices with their start and end apart: 5, of which 3 were waited for; matrix products, arithmetic and copies ran while one was open for 0% of the time, Pallas kernels for 3%

profile of v4, /device:TPU:1, one launch (start us, length us, event | category | flops | bytes accessed | tf_op | source)
XLA Modules:
  0.0 118.5 jit_solution(16574313081078981758)
XLA Ops:
  0.0 1.5 %constant_dynamic-update-slice_fusion.1 = bf16[384,2304]{1,0:T(8,128)(2,1)S(1)} fusion(bf16[384,1792]{1,0:T(8,128)(2,1)} %param.4), kind=kLoop, calls=%fused_computation.3 | loop fusion | bytes 2752512
  1.5 0.0 copy-done.7
  1.5 8.8 %collective-permute-start.2 = (bf16[384,2304]{1,0:T(8,128)(2,1)S(1)}, bf16[384,2304]{1,0:T(8,128)(2,1)S(1)}, u32[]{:S(2)}, u32[]{:S(2)}) collective-permute-start(bf16[384,2304]{1,0:T(8,128)(2,1)S(1)} %constant_dynamic-update-slice_fusion.refs_2_), channel_id=1, source_target_pairs={{0,16},{16,0},{1,17},{17,1},{2,18},{18,2},{3,19},{19,3},{4,20},{20... | collective-permute-start | bytes 5308424 | tf_op jit(solution)/shard_map/ppermute | solution.py:187
  10.3 0.0 copy-done.6
  10.3 0.0 copy-done.5
  10.4 0.2 shard_map.46
  10.6 34.3 %all-gather.1 = f16[256,2432]{1,0:T(8,128)(2,1)S(1)} all-gather(f16[32,2432]{1,0:T(8,128)(2,1)S(1)} %convert_element_type.9), channel_id=1, replica_groups=mesh['zh'=8,'zp'=2,'c'=2,'x'=4,'y'=4] {'zh'}, dimensions={0}, use_global_device_ids=true | all-gather | bytes 1400832 | tf_op jit(solution)/shard_map/all_gather | solution.py:191
  44.8 0.1 slice_convert_fusion
  45.0 0.0 copy-start.3
  45.0 0.0 copy-start.4
  45.0 0.0 collective-permute-done.2.refs_3_
  45.0 0.0 copy-start
  45.0 1.8 %shard_map.47 = f32[256,1664]{1,0:T(8,128)S(1)} custom-call(bf16[128,2432]{1,0:T(8,128)(2,1)S(1)} %get-tuple-element.14.refs_0_, bf16[128,2432]{1,0:T(8,128)(2,1)S(1)} %get-tuple-element.13.refs_1_, bf16[384,2304]{1,0:T(8,128)(2,1)S(1)} %constant_dynamic-update-slice_fusion.refs_2_, bf16[384,2304]{1,0:T(8,128)(2,1)S(1)} %collective-permute-done.2.refs_3_), custom_call_target="tpu_custom_call" | custom-call | flops 20719861760 | bytes 24903680 | tf_op jit(solution)/shard_map/pallas_call | solution.py:98
  46.8 0.0 copy-done.3
  46.8 0.0 copy-done.4
  46.9 0.0 copy-done
  46.9 0.0 copy-start.2
  46.9 1.2 copy-done.2
  48.1 6.4 %all-to-all-start = ((f32[16,16,1664]{2,1,0:T(8,128)}), f32[16,16,1664]{2,1,0:T(8,128)S(1)}, u32[]{:S(2)}, u32[]{:S(2)}) async-start(f32[16,16,1664]{2,1,0:T(8,128)} %bitcast.5), calls=%async_computation | async-start | bytes 3407872 | tf_op jit(solution)/shard_map/all_to_all | solution.py:198
  54.5 1.9 %collective-permute-start.1 = (bf16[128,2432]{1,0:T(8,128)(2,1)}, bf16[128,2432]{1,0:T(8,128)(2,1)S(1)}, u32[]{:S(2)}, u32[]{:S(2)}) collective-permute-start(bf16[128,2432]{1,0:T(8,128)(2,1)} %copy-done.4), channel_id=1, source_target_pairs={{480,0},{0,32},{32,64},{64,96},{96,128},{128,160},{160,192},{192,2... | collective-permute-start | bytes 1867784 | tf_op jit(solution)/shard_map/ppermute | solution.py:184
  56.4 4.6 %collective-permute-start = (bf16[128,2432]{1,0:T(8,128)(2,1)}, bf16[128,2432]{1,0:T(8,128)(2,1)S(1)}, u32[]{:S(2)}, u32[]{:S(2)}) collective-permute-start(bf16[128,2432]{1,0:T(8,128)(2,1)} %copy-done.3), channel_id=1, source_target_pairs={{32,0},{64,32},{96,64},{128,96},{160,128},{192,160},{224,192},{256... | collective-permute-start | bytes 1867784 | tf_op jit(solution)/shard_map/ppermute | solution.py:184
  61.0 6.8 %collective-permute-done.1.refs_1_ = bf16[128,2432]{1,0:T(8,128)(2,1)S(1)} collective-permute-done((bf16[128,2432]{1,0:T(8,128)(2,1)}, bf16[128,2432]{1,0:T(8,128)(2,1)S(1)}, u32[]{:S(2)}, u32[]{:S(2)}) %collective-permute-start.1) | collective-permute-done | bytes 622624 | tf_op jit(solution)/shard_map/ppermute | solution.py:184
  67.8 1.0 collective-permute-done.refs_0_
  68.8 1.5 %copy-done.1 = bf16[384,2304]{1,0:T(8,128)(2,1)S(1)} copy-done((bf16[384,2304]{1,0:T(8,128)(2,1)S(1)}, bf16[384,2304]{1,0:T(8,128)(2,1)}, u32[]{:S(2)}) %copy-start.1) | copy-done | bytes 1769496
  70.3 3.0 %shard_map.48 = f32[256,1664]{1,0:T(8,128)} custom-call(bf16[128,2432]{1,0:T(8,128)(2,1)S(1)} %collective-permute-done.refs_0_, bf16[128,2432]{1,0:T(8,128)(2,1)S(1)} %collective-permute-done.1.refs_1_, bf16[384,2304]{1,0:T(8,128)(2,1)S(1)} %constant_dynamic-update-slice_fusion.refs_2_, bf16[384,2304]{1,0:T(8,128)(2,1)S(1)} %copy-done.1), custom_call_target="tpu_custom_call" | custom-call | flops 10359930 | bytes 12451 | tf_op jit(solution)/shard_map/pallas_call | solution.py:98
  73.3 0.0 all-to-all-done.refs_0_
  73.3 6.3 %all-to-all-start.1 = ((f32[16,16,1664]{2,1,0:T(8,128)}), f32[16,16,1664]{2,1,0:T(8,128)S(1)}, u32[]{:S(2)}, u32[]{:S(2)}) async-start(f32[16,16,1664]{2,1,0:T(8,128)} %bitcast.4), calls=%async_computation.1 | async-start | bytes 3407872 | tf_op jit(solution)/shard_map/all_to_all | solution.py:198
  79.6 0.1 pad_add_fusion.place_ref
  79.7 16.2 %all-to-all-done.1.refs_1_ = f32[16,16,1664]{2,1,0:T(8,128)S(1)} async-done(((f32[16,16,1664]{2,1,0:T(8,128)}), f32[16,16,1664]{2,1,0:T(8,128)S(1)}, u32[]{:S(2)}, u32[]{:S(2)}) %all-to-all-start.1) | async-done | bytes 1703968 | tf_op jit(solution)/shard_map/all_to_all | solution.py:198
  95.9 0.8 shard_map.49
  96.7 21.0 %all_to_all.15.got_ref = f32[32,2,512]{2,1,0:T(2,128)S(1)} all-to-all(f32[32,2,512]{2,1,0:T(2,128)S(1)} %shard_map.49), channel_id=1, replica_groups=mesh['zh'=8,'zp'=2,'c'=2,'x'=4,'y'=4] {'c','x','y'}, dimensions={0} | all-to-all | bytes 262144 | tf_op jit(solution)/shard_map/all_to_all | solution.py:216
  117.7 0.7 shard_map.50
  (6 shorter events, 0.1 us)
Async XLA Ops:
  0.0 1.5 %copy-start.7 = (bf16[384,512]{1,0:T(8,128)(2,1)S(1)}, bf16[384,512]{1,0:T(8,128)(2,1)}, u32[]{:S(2)}) copy-start(bf16[384,512]{1,0:T(8,128)(2,1)} %param.5) | copy-start | bytes 1179652
  0.0 10.3 %copy-start.6 = (bf16[32,512]{1,0:T(8,128)(2,1)S(1)}, bf16[32,512]{1,0:T(8,128)(2,1)}, u32[]{:S(2)}) copy-start(bf16[32,512]{1,0:T(8,128)(2,1)} %right_ref.1) | copy-start | bytes 98308
  0.0 10.3 %copy-start.5 = (bf16[32,1792]{1,0:T(8,128)(2,1)S(1)}, bf16[32,1792]{1,0:T(8,128)(2,1)}, u32[]{:S(2)}) copy-start(bf16[32,1792]{1,0:T(8,128)(2,1)} %left_ref.1) | copy-start | bytes 344068
  1.5 43.5 %collective-permute-start.2 = (bf16[384,2304]{1,0:T(8,128)(2,1)S(1)}, bf16[384,2304]{1,0:T(8,128)(2,1)S(1)}, u32[]{:S(2)}, u32[]{:S(2)}) collective-permute-start(bf16[384,2304]{1,0:T(8,128)(2,1)S(1)} %constant_dynamic-update-slice_fusion.refs_2_), channel_id=1, source_target_pairs={{0,16},{16,0},{1,17},{17,1},{2,18},{18,2},{3,19},{19,3},{4,20},{20... | collective-permute-start | bytes 5308424 | tf_op jit(solution)/shard_map/ppermute | solution.py:187
  45.0 1.9 %copy-start.3 = (bf16[128,2432]{1,0:T(8,128)(2,1)}, bf16[128,2432]{1,0:T(8,128)(2,1)S(1)}, u32[]{:S(2)}) copy-start(bf16[128,2432]{1,0:T(8,128)(2,1)S(1)} %get-tuple-element.14.refs_0_) | copy-start | bytes 1867780
  45.0 1.9 %copy-start.4 = (bf16[128,2432]{1,0:T(8,128)(2,1)}, bf16[128,2432]{1,0:T(8,128)(2,1)S(1)}, u32[]{:S(2)}) copy-start(bf16[128,2432]{1,0:T(8,128)(2,1)S(1)} %get-tuple-element.13.refs_1_) | copy-start | bytes 1867780
  45.0 1.9 %copy-start = (bf16[384,2304]{1,0:T(8,128)(2,1)}, bf16[384,2304]{1,0:T(8,128)(2,1)S(1)}, u32[]{:S(2)}) copy-start(bf16[384,2304]{1,0:T(8,128)(2,1)S(1)} %collective-permute-done.2.refs_3_) | copy-start | bytes 5308420
  46.9 1.2 %copy-start.2 = (f32[256,1664]{1,0:T(8,128)}, f32[256,1664]{1,0:T(8,128)S(1)}, u32[]{:S(2)}) copy-start(f32[256,1664]{1,0:T(8,128)S(1)} %shard_map.47) | copy-start | bytes 5111812
  48.1 25.2 %all-to-all-start = ((f32[16,16,1664]{2,1,0:T(8,128)}), f32[16,16,1664]{2,1,0:T(8,128)S(1)}, u32[]{:S(2)}, u32[]{:S(2)}) async-start(f32[16,16,1664]{2,1,0:T(8,128)} %bitcast.5), calls=%async_computation | async-start | bytes 3407872 | tf_op jit(solution)/shard_map/all_to_all | solution.py:198
  54.5 13.3 %collective-permute-start.1 = (bf16[128,2432]{1,0:T(8,128)(2,1)}, bf16[128,2432]{1,0:T(8,128)(2,1)S(1)}, u32[]{:S(2)}, u32[]{:S(2)}) collective-permute-start(bf16[128,2432]{1,0:T(8,128)(2,1)} %copy-done.4), channel_id=1, source_target_pairs={{480,0},{0,32},{32,64},{64,96},{96,128},{128,160},{160,192},{192,2... | collective-permute-start | bytes 1867784 | tf_op jit(solution)/shard_map/ppermute | solution.py:184
  56.4 12.4 %collective-permute-start = (bf16[128,2432]{1,0:T(8,128)(2,1)}, bf16[128,2432]{1,0:T(8,128)(2,1)S(1)}, u32[]{:S(2)}, u32[]{:S(2)}) collective-permute-start(bf16[128,2432]{1,0:T(8,128)(2,1)} %copy-done.3), channel_id=1, source_target_pairs={{32,0},{64,32},{96,64},{128,96},{160,128},{192,160},{224,192},{256... | collective-permute-start | bytes 1867784 | tf_op jit(solution)/shard_map/ppermute | solution.py:184
  68.8 1.5 %copy-start.1 = (bf16[384,2304]{1,0:T(8,128)(2,1)S(1)}, bf16[384,2304]{1,0:T(8,128)(2,1)}, u32[]{:S(2)}) copy-start(bf16[384,2304]{1,0:T(8,128)(2,1)} %copy-done) | copy-start | bytes 5308420
  73.3 22.6 %all-to-all-start.1 = ((f32[16,16,1664]{2,1,0:T(8,128)}), f32[16,16,1664]{2,1,0:T(8,128)S(1)}, u32[]{:S(2)}, u32[]{:S(2)}) async-start(f32[16,16,1664]{2,1,0:T(8,128)} %bitcast.4), calls=%async_computation.1 | async-start | bytes 3407872 | tf_op jit(solution)/shard_map/all_to_all | solution.py:198

commit v5 on v4

--- a/solution.py
+++ b/solution.py
@@ -8,10 +8,11 @@
 
 R = 32
 GROUP = 128
+OWNERS = 16
 CLASSES = 2
 TOP = 2.0**15
 POWERS = (64, 32, 16, 8, 4, 2, 1)
-WEIGHTS = (20, 0.01)
+WEIGHTS = (1, 0.01)
 
 epsilon = 1e-06
 
@@ -72,7 +73,9 @@
     rows = sum(p.shape[0] for p in pieces)
     packed = pieces[0].shape[1]
     own, both = mine.shape
-    width = 4 * own + GROUP
+    half = 4 * own
+    width = 2 * half + GROUP
+    share = rows // OWNERS
 
     def body(*refs):
         q_refs, (mine_ref, theirs_ref, out, left, right) = refs[: len(pieces)], refs[len(pieces) :]
@@ -83,71 +86,107 @@
             left[here] = unscaled(q_ref[:, :wide], exponents[:, 0:1])
             right[here] = unscaled(q_ref[:, wide:both], exponents[:, 1:2])
             at += q_ref.shape[0]
-        out[:, :own] = dot(left[...], mine_ref[:, :wide])
-        out[:, own : 2 * own] = dot(left[...], theirs_ref[:, :wide])
-        out[:, 2 * own : 3 * own] = dot(right[...], mine_ref[:, wide:])
-        out[:, 3 * own : 4 * own] = dot(right[...], theirs_ref[:, wide:])
+        for at, factors, tokens in (
+            (0, left, mine_ref[:, :wide]),
+            (own, left, theirs_ref[:, :wide]),
+            (2 * own, right, mine_ref[:, wide:]),
+            (3 * own, right, theirs_ref[:, wide:]),
+        ):
+            value = dot(factors[...], tokens).reshape(OWNERS, share, own)
+            out[:, :, at : at + own] = value[:, : share // 2]
+            out[:, :, half + at : half + at + own] = value[:, share // 2 :]
         query = lax.broadcasted_iota(jnp.int32, (GROUP, GROUP), 0) // R
         block = lax.broadcasted_iota(jnp.int32, (GROUP, GROUP), 1) // R
-        for at in range(0, rows, GROUP):
-            here = slice(at, at + GROUP)
+        count = GROUP // share
+        shape = (count, share // 2, GROUP)
+        first = lax.broadcasted_iota(jnp.int32, shape, 0) * share // R
+        ahead = lax.rem(lax.broadcasted_iota(jnp.int32, shape, 2) // R - first + GROUP // R, GROUP // R)
+        for i in range(rows // GROUP):
+            here = slice(i * GROUP, (i + 1) * GROUP)
             x, y = left[here], right[here]
             next_y = jnp.concatenate([y[GROUP - R :], y[: GROUP - R]], axis=0)
-            out[here, 4 * own :] = jnp.where(query == block, dot(x, x), dot(y, next_y))
+            gram = jnp.where(query == block, dot(x, x), dot(y, next_y))
+            moved = pltpu.roll(gram, 2 * R, 1).reshape(count, share, GROUP)
+            gram = gram.reshape(count, share, GROUP)
+            out[i * count : (i + 1) * count, :, 2 * half :] = jnp.where(
+                ahead < 2, gram[:, : share // 2], moved[:, share // 2 :]
+            )
 
     return pl.pallas_call(
         body,
         in_specs=[VMEM] * (len(pieces) + 2),
         out_specs=VMEM,
-        out_shape=jax.ShapeDtypeStruct((rows, width), jnp.float32),
+        out_shape=jax.ShapeDtypeStruct((OWNERS, share // 2, width), jnp.float32),
         scratch_shapes=[
             pltpu.VMEM((rows, wide), mine.dtype),
             pltpu.VMEM((rows, both - wide), mine.dtype),
         ],
         compiler_params=params(),
         cost_estimate=pl.CostEstimate(
-            flops=int(weight * rows * width * packed),
+            flops=int(weight * rows * half * packed),
             bytes_accessed=int(weight * 2 * rows * packed),
             transcendentals=0,
         ),
     )(*pieces, mine, theirs)
 
 
-def finish(place, parts):
-    owners = parts[0].shape[0]
-    own = (parts[0].shape[2] - GROUP) // 4
-
-    def body(place_ref, *refs):
-        out = refs[-1]
-        core, parity, slot = place_ref[0], place_ref[1], place_ref[2]
-        lanes = lax.broadcasted_iota(jnp.int32, (1, GROUP), 1)
-        at = lax.broadcasted_iota(jnp.int32, (CLASSES, own + GROUP), 0)
-        mine = jnp.zeros((CLASSES, own + GROUP), jnp.float32)
-        theirs = mine
-        for k, ref in enumerate(refs[:-1]):
-            total = ref[0]
-            for s in range(1, owners):
-                total = total + ref[s]
-            both = jnp.sum(total[:, : 2 * own] * total[:, 2 * own : 4 * own], axis=0, keepdims=True)
-            gram = total[:, 4 * own :]
-            gram = gram * pltpu.roll(gram, GROUP - R, 1)
-            square = jnp.sum(jnp.where(lanes // R == slot, gram, 0.0), axis=(0, 1), keepdims=True)
-            square = jnp.broadcast_to(square, (1, GROUP))
-            row = at == lax.rem(parity + k, CLASSES)
-            mine = jnp.where(row, jnp.concatenate([both[:, :own], square], 1), mine)
-            theirs = jnp.where(row, jnp.concatenate([both[:, own:], square], 1), theirs)
-        first = jnp.where(core == 0, mine, theirs)
-        second = jnp.where(core == 0, theirs, mine)
-        out[:owners] = jnp.broadcast_to(first[None], (owners, *first.shape))
-        out[owners:] = jnp.broadcast_to(second[None], (owners, *second.shape))
-
-    return pl.pallas_call(
-        body,
-        in_specs=[SMEM] + [VMEM] * len(parts),
-        out_specs=VMEM,
-        out_shape=jax.ShapeDtypeStruct((2 * owners, CLASSES, own + GROUP), jnp.float32),
-        compiler_params=params(),
-    )(place, *parts)
+def class_rows(place, terms):
+    half = (terms.shape[2] - GROUP) // 2
+    own = half // 4
+    total = terms[0]
+    for s in range(1, OWNERS):
+        total = total + terms[s]
+    products = total[:, : 2 * own] * total[:, 2 * own : half]
+    products += total[:, half : half + 2 * own] * total[:, half + 2 * own : 2 * half]
+    both = jnp.sum(products, axis=0, keepdims=True)
+    gram = total[:, 2 * half :]
+    gram = gram * pltpu.roll(gram, GROUP - R, 1)
+    lanes = lax.broadcasted_iota(jnp.int32, (1, GROUP), 1)
+    lefts = lax.rem(lanes // R + place[2], 2) == 0
+    square = jnp.sum(jnp.where(lefts, gram, 0.0), axis=(0, 1), keepdims=True)
+    square = jnp.broadcast_to(square, (1, GROUP))
+    mine = jnp.concatenate([both[:, :own], square], axis=1)
+    theirs = jnp.concatenate([both[:, own:], square], axis=1)
+    return jnp.where(place[0] == 0, mine, theirs), jnp.where(place[0] == 0, theirs, mine)
+
+
+def finish_first(place, terms):
+    width = (terms.shape[2] - GROUP) // 8 + GROUP
+
+    def body(place_ref, terms_ref, out):
+        out[0:1], out[1:2] = class_rows(place_ref, terms_ref)
+
+    return pl.pallas_call(
+        body,
+        in_specs=[SMEM, VMEM],
+        out_specs=VMEM,
+        out_shape=jax.ShapeDtypeStruct((2, width), jnp.float32),
+        compiler_params=params(),
+        cost_estimate=pl.CostEstimate(
+            flops=10_000_000_000, bytes_accessed=4 * terms.size, transcendentals=0
+        ),
+    )(place, terms)
+
+
+def finish(place, first_rows, terms):
+    width = first_rows.shape[1]
+
+    def body(place_ref, first_ref, terms_ref, out):
+        second = class_rows(place_ref, terms_ref)
+        at = lax.broadcasted_iota(jnp.int32, (CLASSES, width), 0)
+        for core in range(2):
+            rows = jnp.where(at == place_ref[1], first_ref[core : core + 1], second[core])
+            out[core * OWNERS : (core + 1) * OWNERS] = jnp.broadcast_to(
+                rows[None], (OWNERS, CLASSES, width)
+            )
+
+    return pl.pallas_call(
+        body,
+        in_specs=[SMEM, VMEM, VMEM],
+        out_specs=VMEM,
+        out_shape=jax.ShapeDtypeStruct((2 * OWNERS, CLASSES, width), jnp.float32),
+        compiler_params=params(),
+    )(place, first_rows, terms)
 
 
 def scores_of(got, shares):
@@ -177,7 +216,6 @@
 
 def on_device(hidden_acts, out_grads, query_left, query_right):
     planes = lax.axis_size(("zh", "zp"))
-    owners = lax.axis_size(("x", "y"))
 
     def from_plane(block, ahead):
         pairs = [((z + ahead) % planes, z) for z in range(planes)]
@@ -194,16 +232,9 @@
     there = (from_plane(here[0], 1), from_plane(here[1], -1))
 
     def owned(terms):
-        terms = terms.reshape(owners, terms.shape[0] // owners, terms.shape[1])
         return lax.all_to_all(terms, ("x", "y"), split_axis=0, concat_axis=0, tiled=True)
 
-    first_terms = project(WEIGHTS[0], wide, here, *tokens)
-    first = owned(first_terms)
-    there, _ = lax.optimization_barrier((there, first_terms))
-    second_terms, first = lax.optimization_barrier((project(WEIGHTS[1], wide, there, *tokens), first))
-    second = owned(second_terms)
-
-    share = 2 * half // owners
+    share = 2 * half // OWNERS
     shares = R // share
     place = jnp.stack(
         [
@@ -212,7 +243,13 @@
             lax.rem(lax.axis_index(("x", "y")) // shares, GROUP // R),
         ]
     ).astype(jnp.int32)
-    sums = finish(place, (first, second))
+
+    first_terms = project(WEIGHTS[0], wide, here, *tokens)
+    first = owned(first_terms)
+    there, _ = lax.optimization_barrier((there, first_terms))
+    second_terms, first = lax.optimization_barrier((project(WEIGHTS[1], wide, there, *tokens), first))
+    second = owned(second_terms)
+    sums = finish(place, finish_first(place, first), second)
     got = lax.all_to_all(sums, ("c", "x", "y"), split_axis=0, concat_axis=0, tiled=True)
     return scores_of(got, shares)
 

time: 119 us -> 118 us (level)
  waiting for transfers between devices: 24 us -> 22 us
    all_to_all x2, waiting for transfers between devices: 16.2 us -> 14.1 us  [owned(): lax.all_to_all(terms, ('x', 'y'), split_axis=0, concat_axis=0, tiled=True)]
    pallas_call x1 -> x2, Pallas kernels: 0.79 us -> 2.4 us  [the longest x1 1.65 us: finish_first(): pl.pallas_call(body, in_specs=[SMEM, VMEM], out_specs=VMEM, out_shape=jax...]
    unnamed x17 -> x15, local copies, waits for them, and re-layouts: 4.16 us -> 4.9 us
  transfers between devices with their start and end apart: 5 -> 5, of which waited for: 3 -> 4; matrix products, arithmetic and copies ran while one was open for 0% -> 0% of each run, Pallas kernels for 3% -> 3%
where the time goes in v5:
time: 118 us; the launch traced here: 117 us
  blocking collectives  54.9 us (47%)
  starting transfers between devices  28 us (24%)
  waiting for transfers between devices  22 us (19%)
  Pallas kernels  7.05 us (6%)
  local copies, waits for them, and re-layouts  4.93 us (4%)
    all_gather x1, blocking collectives, on_device(): here = lax.all_gather(sent, 'zh', axis=0, tiled=True)  34.3 us
    all_to_all x1, blocking collectives, on_device(): lax.all_to_all(sums, ('c', 'x', 'y'), split_axis=0, concat_axis=0, tiled=...  20.6 us
    all_to_all x2, waiting for transfers between devices, owned(): lax.all_to_all(terms, ('x', 'y'), split_axis=0, concat_axis=0, tiled=True)  14.1 us
    all_to_all x2, starting transfers between devices, owned(): lax.all_to_all(terms, ('x', 'y'), split_axis=0, concat_axis=0, tiled=True)  12.7 us
    ppermute x1, starting transfers between devices, on_device(): tokens = (mine, lax.ppermute(mine, 'c', [(0, 1), (1, 0)]))  8.78 us
    ppermute x2, waiting for transfers between devices, from_plane(): return lax.ppermute(block, ('zh', 'zp'), pairs)  7.86 us
    ppermute x2, starting transfers between devices, from_plane(): return lax.ppermute(block, ('zh', 'zp'), pairs)  6.49 us
    unnamed x15, local copies, waits for them, and re-layouts  4.9 us
  transfers between devices with their start and end apart: 5, of which 4 were waited for; matrix products, arithmetic and copies ran while one was open for 0% of the time, Pallas kernels for 3%

profile of v5, /device:TPU:1, one launch (start us, length us, event | category | flops | bytes accessed | tf_op | source)
XLA Modules:
  0.0 117.2 jit_solution(9342763694894659730)
XLA Ops:
  0.0 0.0 copy-start.6
  0.0 0.0 copy-start.5
  0.0 1.5 %constant_dynamic-update-slice_fusion.1 = bf16[384,2304]{1,0:T(8,128)(2,1)S(1)} fusion(bf16[384,1792]{1,0:T(8,128)(2,1)} %param.4), kind=kLoop, calls=%fused_computation.3 | loop fusion | bytes 2752512
  1.5 0.0 copy-done.6
  1.5 8.8 %collective-permute-start.2 = (bf16[384,2304]{1,0:T(8,128)(2,1)S(1)}, bf16[384,2304]{1,0:T(8,128)(2,1)S(1)}, u32[]{:S(2)}, u32[]{:S(2)}) collective-permute-start(bf16[384,2304]{1,0:T(8,128)(2,1)S(1)} %constant_dynamic-update-slice_fusion.refs_2_), channel_id=1, source_target_pairs={{0,16},{16,0},{1,17},{17,1},{2,18},{18,2},{3,19},{19,3},{4,20},{20... | collective-permute-start | bytes 5308424 | tf_op jit(solution)/shard_map/ppermute | solution.py:225
  10.3 0.0 copy-done.5
  10.3 0.0 copy-done.4
  10.4 0.2 shard_map.46
  10.6 34.3 %all-gather.1 = f16[256,2432]{1,0:T(8,128)(2,1)S(1)} all-gather(f16[32,2432]{1,0:T(8,128)(2,1)S(1)} %convert_element_type.9), channel_id=1, replica_groups=mesh['zh'=8,'zp'=2,'c'=2,'x'=4,'y'=4] {'zh'}, dimensions={0}, use_global_device_ids=true | all-gather | bytes 1400832 | tf_op jit(solution)/shard_map/all_gather | solution.py:229
  44.8 0.1 slice_convert_fusion
  45.0 0.0 copy-start.2
  45.0 0.0 copy-start.3
  45.0 0.0 collective-permute-done.2.refs_3_
  45.0 0.8 copy-done.2
  45.8 0.2 copy-done.3
  46.0 1.9 %shard_map.47 = f32[16,8,3200]{2,1,0:T(8,128)S(1)} custom-call(bf16[128,2432]{1,0:T(8,128)(2,1)S(1)} %get-tuple-element.14.refs_0_, bf16[128,2432]{1,0:T(8,128)(2,1)S(1)} %get-tuple-element.13.refs_1_, bf16[384,2304]{1,0:T(8,128)(2,1)S(1)} %constant_dynamic-update-slice_fusion.refs_2_, bf16[384,2304]{1,0:T(8,128)(2,1)S(1)} %collective-permute-done.2.refs_3_), custom_call_target="tpu_custom_call" | custom-call | flops 956301312 | bytes 1245184 | tf_op jit(solution)/shard_map/pallas_call | solution.py:115
  47.9 1.2 %copy-done.1 = f32[16,8,3200]{2,1,0:T(8,128)} copy-done((f32[16,8,3200]{2,1,0:T(8,128)}, f32[16,8,3200]{2,1,0:T(8,128)S(1)}, u32[]{:S(2)}) %copy-start.1) | copy-done | bytes 1638424
  49.1 6.4 %all-to-all-start = ((f32[16,8,3200]{2,1,0:T(8,128)}), f32[16,8,3200]{2,1,0:T(8,128)}, u32[]{:S(2)}, u32[]{:S(2)}) async-start(f32[16,8,3200]{2,1,0:T(8,128)} %copy-done.1), calls=%async_computation | async-start | bytes 3276800 | tf_op jit(solution)/shard_map/all_to_all | solution.py:235
  55.6 1.9 %collective-permute-start.1 = (bf16[128,2432]{1,0:T(8,128)(2,1)}, bf16[128,2432]{1,0:T(8,128)(2,1)S(1)}, u32[]{:S(2)}, u32[]{:S(2)}) collective-permute-start(bf16[128,2432]{1,0:T(8,128)(2,1)} %copy-done.3), channel_id=1, source_target_pairs={{480,0},{0,32},{32,64},{64,96},{96,128},{128,160},{160,192},{192,2... | collective-permute-start | bytes 1867784 | tf_op jit(solution)/shard_map/ppermute | solution.py:222
  57.5 4.6 %collective-permute-start = (bf16[128,2432]{1,0:T(8,128)(2,1)}, bf16[128,2432]{1,0:T(8,128)(2,1)S(1)}, u32[]{:S(2)}, u32[]{:S(2)}) collective-permute-start(bf16[128,2432]{1,0:T(8,128)(2,1)} %copy-done.2), channel_id=1, source_target_pairs={{32,0},{64,32},{96,64},{128,96},{160,128},{192,160},{224,192},{256... | collective-permute-start | bytes 1867784 | tf_op jit(solution)/shard_map/ppermute | solution.py:222
  62.1 6.9 %collective-permute-done.1.refs_1_ = bf16[128,2432]{1,0:T(8,128)(2,1)S(1)} collective-permute-done((bf16[128,2432]{1,0:T(8,128)(2,1)}, bf16[128,2432]{1,0:T(8,128)(2,1)S(1)}, u32[]{:S(2)}, u32[]{:S(2)}) %collective-permute-start.1) | collective-permute-done | bytes 622624 | tf_op jit(solution)/shard_map/ppermute | solution.py:222
  69.0 0.9 collective-permute-done.refs_0_
  70.0 1.9 %shard_map.48 = f32[16,8,3200]{2,1,0:T(8,128)S(1)} custom-call(bf16[128,2432]{1,0:T(8,128)(2,1)S(1)} %collective-permute-done.refs_0_, bf16[128,2432]{1,0:T(8,128)(2,1)S(1)} %collective-permute-done.1.refs_1_, bf16[384,2304]{1,0:T(8,128)(2,1)S(1)} %constant_dynamic-update-slice_fusion.refs_2_, bf16[384,2304]{1,0:T(8,128)(2,1)S(1)} %collective-permute-done.2.refs_3_), custom_call_target="tpu_custom_call" | custom-call | flops 9563013 | bytes 12451 | tf_op jit(solution)/shard_map/pallas_call | solution.py:115
  71.8 1.2 copy-done
  73.0 0.1 all-to-all-done.terms_ref
  73.1 6.2 %all-to-all-start.1 = ((f32[16,8,3200]{2,1,0:T(8,128)}), f32[16,8,3200]{2,1,0:T(8,128)S(1)}, u32[]{:S(2)}, u32[]{:S(2)}) async-start(f32[16,8,3200]{2,1,0:T(8,128)} %copy-done), calls=%async_computation.1 | async-start | bytes 3276800 | tf_op jit(solution)/shard_map/all_to_all | solution.py:235
  79.4 0.1 pad_add_fusion.place_ref
  79.4 1.6 %shard_map.49.first_ref = f32[2,512]{1,0:T(2,128)S(1)} custom-call(s32[3]{0:T(128)S(1)} %pad_add_fusion.place_ref, f32[16,8,3200]{2,1,0:T(8,128)} %all-to-all-done.terms_ref), custom_call_target="tpu_custom_call" | custom-call | flops 10000000000 | bytes 1638400 | tf_op jit(solution)/shard_map/pallas_call | solution.py:159
  81.1 14.0 %all-to-all-done.1.terms_ref = f32[16,8,3200]{2,1,0:T(8,128)S(1)} async-done(((f32[16,8,3200]{2,1,0:T(8,128)}), f32[16,8,3200]{2,1,0:T(8,128)S(1)}, u32[]{:S(2)}, u32[]{:S(2)}) %all-to-all-start.1) | async-done | bytes 1638432 | tf_op jit(solution)/shard_map/all_to_all | solution.py:235
  95.1 0.8 shard_map.50
  95.8 20.6 %all_to_all.15.got_ref = f32[32,2,512]{2,1,0:T(2,128)S(1)} all-to-all(f32[32,2,512]{2,1,0:T(2,128)S(1)} %shard_map.50), channel_id=1, replica_groups=mesh['zh'=8,'zp'=2,'c'=2,'x'=4,'y'=4] {'c','x','y'}, dimensions={0} | all-to-all | bytes 262144 | tf_op jit(solution)/shard_map/all_to_all | solution.py:253
  116.5 0.7 shard_map.51
  (5 shorter events, 0.1 us)
Async XLA Ops:
  0.0 1.5 %copy-start.6 = (bf16[384,512]{1,0:T(8,128)(2,1)S(1)}, bf16[384,512]{1,0:T(8,128)(2,1)}, u32[]{:S(2)}) copy-start(bf16[384,512]{1,0:T(8,128)(2,1)} %param.5) | copy-start | bytes 1179652
  0.0 10.3 %copy-start.5 = (bf16[32,512]{1,0:T(8,128)(2,1)S(1)}, bf16[32,512]{1,0:T(8,128)(2,1)}, u32[]{:S(2)}) copy-start(bf16[32,512]{1,0:T(8,128)(2,1)} %right_ref.1) | copy-start | bytes 98308
  0.0 10.3 %copy-start.4 = (bf16[32,1792]{1,0:T(8,128)(2,1)S(1)}, bf16[32,1792]{1,0:T(8,128)(2,1)}, u32[]{:S(2)}) copy-start(bf16[32,1792]{1,0:T(8,128)(2,1)} %left_ref.1) | copy-start | bytes 344068
  1.5 43.5 %collective-permute-start.2 = (bf16[384,2304]{1,0:T(8,128)(2,1)S(1)}, bf16[384,2304]{1,0:T(8,128)(2,1)S(1)}, u32[]{:S(2)}, u32[]{:S(2)}) collective-permute-start(bf16[384,2304]{1,0:T(8,128)(2,1)S(1)} %constant_dynamic-update-slice_fusion.refs_2_), channel_id=1, source_target_pairs={{0,16},{16,0},{1,17},{17,1},{2,18},{18,2},{3,19},{19,3},{4,20},{20... | collective-permute-start | bytes 5308424 | tf_op jit(solution)/shard_map/ppermute | solution.py:225
  45.0 0.8 copy-start.2
  45.0 1.0 copy-start.3
  47.9 1.2 %copy-start.1 = (f32[16,8,3200]{2,1,0:T(8,128)}, f32[16,8,3200]{2,1,0:T(8,128)S(1)}, u32[]{:S(2)}) copy-start(f32[16,8,3200]{2,1,0:T(8,128)S(1)} %shard_map.47) | copy-start | bytes 4915204
  49.1 24.0 %all-to-all-start = ((f32[16,8,3200]{2,1,0:T(8,128)}), f32[16,8,3200]{2,1,0:T(8,128)}, u32[]{:S(2)}, u32[]{:S(2)}) async-start(f32[16,8,3200]{2,1,0:T(8,128)} %copy-done.1), calls=%async_computation | async-start | bytes 3276800 | tf_op jit(solution)/shard_map/all_to_all | solution.py:235
  55.6 13.4 %collective-permute-start.1 = (bf16[128,2432]{1,0:T(8,128)(2,1)}, bf16[128,2432]{1,0:T(8,128)(2,1)S(1)}, u32[]{:S(2)}, u32[]{:S(2)}) collective-permute-start(bf16[128,2432]{1,0:T(8,128)(2,1)} %copy-done.3), channel_id=1, source_target_pairs={{480,0},{0,32},{32,64},{64,96},{96,128},{128,160},{160,192},{192,2... | collective-permute-start | bytes 1867784 | tf_op jit(solution)/shard_map/ppermute | solution.py:222
  57.5 12.4 %collective-permute-start = (bf16[128,2432]{1,0:T(8,128)(2,1)}, bf16[128,2432]{1,0:T(8,128)(2,1)S(1)}, u32[]{:S(2)}, u32[]{:S(2)}) collective-permute-start(bf16[128,2432]{1,0:T(8,128)(2,1)} %copy-done.2), channel_id=1, source_target_pairs={{32,0},{64,32},{96,64},{128,96},{160,128},{192,160},{224,192},{256... | collective-permute-start | bytes 1867784 | tf_op jit(solution)/shard_map/ppermute | solution.py:222
  71.8 1.2 %copy-start = (f32[16,8,3200]{2,1,0:T(8,128)}, f32[16,8,3200]{2,1,0:T(8,128)S(1)}, u32[]{:S(2)}) copy-start(f32[16,8,3200]{2,1,0:T(8,128)S(1)} %shard_map.48) | copy-start | bytes 4915204
  73.1 22.0 %all-to-all-start.1 = ((f32[16,8,3200]{2,1,0:T(8,128)}), f32[16,8,3200]{2,1,0:T(8,128)S(1)}, u32[]{:S(2)}, u32[]{:S(2)}) async-start(f32[16,8,3200]{2,1,0:T(8,128)} %copy-done), calls=%async_computation.1 | async-start | bytes 3276800 | tf_op jit(solution)/shard_map/all_to_all | solution.py:235

commit v6 on v5

--- a/solution.py
+++ b/solution.py
@@ -12,7 +12,7 @@
 CLASSES = 2
 TOP = 2.0**15
 POWERS = (64, 32, 16, 8, 4, 2, 1)
-WEIGHTS = (1, 0.01)
+WEIGHTS = (20, 0.01)
 
 epsilon = 1e-06
 

time: 118 us -> 118 us (level)
    unnamed x15 -> x13, local copies, waits for them, and re-layouts: 4.9 us -> 3.72 us
  transfers between devices with their start and end apart: 5 -> 5, of which waited for: 4 -> 4; matrix products, arithmetic and copies ran while one was open for 0% -> 0% of each run, Pallas kernels for 3% -> 4%
where the time goes in v6:
time: 118 us; the launch traced here: 117 us
  blocking collectives  54.9 us (47%)
  starting transfers between devices  28 us (24%)
  waiting for transfers between devices  22 us (19%)
  Pallas kernels  8.22 us (7%)
  local copies, waits for them, and re-layouts  3.75 us (3%)
    all_gather x1, blocking collectives, on_device(): here = lax.all_gather(sent, 'zh', axis=0, tiled=True)  34.3 us
    all_to_all x1, blocking collectives, on_device(): lax.all_to_all(sums, ('c', 'x', 'y'), split_axis=0, concat_axis=0, tiled=...  20.6 us
    all_to_all x2, waiting for transfers between devices, owned(): lax.all_to_all(terms, ('x', 'y'), split_axis=0, concat_axis=0, tiled=True)  14.1 us
    all_to_all x2, starting transfers between devices, owned(): lax.all_to_all(terms, ('x', 'y'), split_axis=0, concat_axis=0, tiled=True)  12.7 us
    ppermute x1, starting transfers between devices, on_device(): tokens = (mine, lax.ppermute(mine, 'c', [(0, 1), (1, 0)]))  8.78 us
    ppermute x2, waiting for transfers between devices, from_plane(): return lax.ppermute(block, ('zh', 'zp'), pairs)  7.88 us
    ppermute x2, starting transfers between devices, from_plane(): return lax.ppermute(block, ('zh', 'zp'), pairs)  6.49 us
    pallas_call x2, Pallas kernels, project(): pl.pallas_call(body, in_specs=[VMEM] * (len(pieces) + 2), out_specs=VMEM,...  4.93 us
  transfers between devices with their start and end apart: 5, of which 4 were waited for; matrix products, arithmetic and copies ran while one was open for 0% of the time, Pallas kernels for 4%

profile of v6, /device:TPU:1, one launch (start us, length us, event | category | flops | bytes accessed | tf_op | source)
XLA Modules:
  0.0 117.2 jit_solution(8231492330096999173)
XLA Ops:
  0.0 0.0 copy-start.5
  0.0 0.0 copy-start.4
  0.0 0.0 copy-start.3
  0.0 1.5 %constant_dynamic-update-slice_fusion.1 = bf16[384,2304]{1,0:T(8,128)(2,1)S(1)} fusion(bf16[384,1792]{1,0:T(8,128)(2,1)} %param.4), kind=kLoop, calls=%fused_computation.3 | loop fusion | bytes 2752512
  1.5 0.0 copy-done.5
  1.5 8.8 %collective-permute-start.2 = (bf16[384,2304]{1,0:T(8,128)(2,1)S(1)}, bf16[384,2304]{1,0:T(8,128)(2,1)S(1)}, u32[]{:S(2)}, u32[]{:S(2)}) collective-permute-start(bf16[384,2304]{1,0:T(8,128)(2,1)S(1)} %constant_dynamic-update-slice_fusion.refs_2_), channel_id=1, source_target_pairs={{0,16},{16,0},{1,17},{17,1},{2,18},{18,2},{3,19},{19,3},{4,20},{20... | collective-permute-start | bytes 5308424 | tf_op jit(solution)/shard_map/ppermute | solution.py:225
  10.3 0.0 copy-done.4
  10.3 0.0 copy-done.3
  10.4 0.2 shard_map.46
  10.6 34.3 %all-gather.1 = f16[256,2432]{1,0:T(8,128)(2,1)S(1)} all-gather(f16[32,2432]{1,0:T(8,128)(2,1)S(1)} %convert_element_type.9), channel_id=1, replica_groups=mesh['zh'=8,'zp'=2,'c'=2,'x'=4,'y'=4] {'zh'}, dimensions={0}, use_global_device_ids=true | all-gather | bytes 1400832 | tf_op jit(solution)/shard_map/all_gather | solution.py:229
  44.8 0.1 slice_convert_fusion
  45.0 0.0 copy-start.1
  45.0 0.0 copy-start.2
  45.0 0.0 collective-permute-done.2.refs_3_
  45.0 0.8 copy-done.1
  45.8 0.2 copy-done.2
  46.0 1.9 %shard_map.47 = f32[16,8,3200]{2,1,0:T(8,128)S(1)} custom-call(bf16[128,2432]{1,0:T(8,128)(2,1)S(1)} %get-tuple-element.14.refs_0_, bf16[128,2432]{1,0:T(8,128)(2,1)S(1)} %get-tuple-element.13.refs_1_, bf16[384,2304]{1,0:T(8,128)(2,1)S(1)} %constant_dynamic-update-slice_fusion.refs_2_, bf16[384,2304]{1,0:T(8,128)(2,1)S(1)} %collective-permute-done.2.refs_3_), custom_call_target="tpu_custom_call" | custom-call | flops 19126026240 | bytes 24903680 | tf_op jit(solution)/shard_map/pallas_call | solution.py:115
  47.9 1.2 %copy-done = f32[16,8,3200]{2,1,0:T(8,128)} copy-done((f32[16,8,3200]{2,1,0:T(8,128)}, f32[16,8,3200]{2,1,0:T(8,128)S(1)}, u32[]{:S(2)}) %copy-start) | copy-done | bytes 1638424
  49.1 6.4 %all-to-all-start = ((f32[16,8,3200]{2,1,0:T(8,128)}), f32[16,8,3200]{2,1,0:T(8,128)}, u32[]{:S(2)}, u32[]{:S(2)}) async-start(f32[16,8,3200]{2,1,0:T(8,128)} %copy-done), calls=%async_computation | async-start | bytes 3276800 | tf_op jit(solution)/shard_map/all_to_all | solution.py:235
  55.6 1.9 %collective-permute-start.1 = (bf16[128,2432]{1,0:T(8,128)(2,1)}, bf16[128,2432]{1,0:T(8,128)(2,1)S(1)}, u32[]{:S(2)}, u32[]{:S(2)}) collective-permute-start(bf16[128,2432]{1,0:T(8,128)(2,1)} %copy-done.2), channel_id=1, source_target_pairs={{480,0},{0,32},{32,64},{64,96},{96,128},{128,160},{160,192},{192,2... | collective-permute-start | bytes 1867784 | tf_op jit(solution)/shard_map/ppermute | solution.py:222
  57.5 4.6 %collective-permute-start = (bf16[128,2432]{1,0:T(8,128)(2,1)}, bf16[128,2432]{1,0:T(8,128)(2,1)S(1)}, u32[]{:S(2)}, u32[]{:S(2)}) collective-permute-start(bf16[128,2432]{1,0:T(8,128)(2,1)} %copy-done.1), channel_id=1, source_target_pairs={{32,0},{64,32},{96,64},{128,96},{160,128},{192,160},{224,192},{256... | collective-permute-start | bytes 1867784 | tf_op jit(solution)/shard_map/ppermute | solution.py:222
  62.1 6.9 %collective-permute-done.1.refs_1_ = bf16[128,2432]{1,0:T(8,128)(2,1)S(1)} collective-permute-done((bf16[128,2432]{1,0:T(8,128)(2,1)}, bf16[128,2432]{1,0:T(8,128)(2,1)S(1)}, u32[]{:S(2)}, u32[]{:S(2)}) %collective-permute-start.1) | collective-permute-done | bytes 622624 | tf_op jit(solution)/shard_map/ppermute | solution.py:222
  69.0 1.0 collective-permute-done.refs_0_
  70.0 3.0 %shard_map.48 = f32[16,8,3200]{2,1,0:T(8,128)} custom-call(bf16[128,2432]{1,0:T(8,128)(2,1)S(1)} %collective-permute-done.refs_0_, bf16[128,2432]{1,0:T(8,128)(2,1)S(1)} %collective-permute-done.1.refs_1_, bf16[384,2304]{1,0:T(8,128)(2,1)S(1)} %constant_dynamic-update-slice_fusion.refs_2_, bf16[384,2304]{1,0:T(8,128)(2,1)S(1)} %collective-permute-done.2.refs_3_), custom_call_target="tpu_custom_call" | custom-call | flops 9563013 | bytes 12451 | tf_op jit(solution)/shard_map/pallas_call | solution.py:115
  73.0 0.1 all-to-all-done.terms_ref
  73.1 6.2 %all-to-all-start.1 = ((f32[16,8,3200]{2,1,0:T(8,128)}), f32[16,8,3200]{2,1,0:T(8,128)S(1)}, u32[]{:S(2)}, u32[]{:S(2)}) async-start(f32[16,8,3200]{2,1,0:T(8,128)} %shard_map.48), calls=%async_computation.1 | async-start | bytes 3276800 | tf_op jit(solution)/shard_map/all_to_all | solution.py:235
  79.4 0.1 pad_add_fusion.place_ref
  79.4 1.6 %shard_map.49.first_ref = f32[2,512]{1,0:T(2,128)S(1)} custom-call(s32[3]{0:T(128)S(1)} %pad_add_fusion.place_ref, f32[16,8,3200]{2,1,0:T(8,128)} %all-to-all-done.terms_ref), custom_call_target="tpu_custom_call" | custom-call | flops 10000000000 | bytes 1638400 | tf_op jit(solution)/shard_map/pallas_call | solution.py:159
  81.1 14.0 %all-to-all-done.1.terms_ref = f32[16,8,3200]{2,1,0:T(8,128)S(1)} async-done(((f32[16,8,3200]{2,1,0:T(8,128)}), f32[16,8,3200]{2,1,0:T(8,128)S(1)}, u32[]{:S(2)}, u32[]{:S(2)}) %all-to-all-start.1) | async-done | bytes 1638432 | tf_op jit(solution)/shard_map/all_to_all | solution.py:235
  95.1 0.8 shard_map.50
  95.8 20.6 %all_to_all.15.got_ref = f32[32,2,512]{2,1,0:T(2,128)S(1)} all-to-all(f32[32,2,512]{2,1,0:T(2,128)S(1)} %shard_map.50), channel_id=1, replica_groups=mesh['zh'=8,'zp'=2,'c'=2,'x'=4,'y'=4] {'c','x','y'}, dimensions={0} | all-to-all | bytes 262144 | tf_op jit(solution)/shard_map/all_to_all | solution.py:253
  116.4 0.7 shard_map.51
  (3 shorter events, 0.1 us)
Async XLA Ops:
  0.0 1.5 %copy-start.5 = (bf16[384,512]{1,0:T(8,128)(2,1)S(1)}, bf16[384,512]{1,0:T(8,128)(2,1)}, u32[]{:S(2)}) copy-start(bf16[384,512]{1,0:T(8,128)(2,1)} %param.5) | copy-start | bytes 1179652
  0.0 10.3 %copy-start.4 = (bf16[32,512]{1,0:T(8,128)(2,1)S(1)}, bf16[32,512]{1,0:T(8,128)(2,1)}, u32[]{:S(2)}) copy-start(bf16[32,512]{1,0:T(8,128)(2,1)} %right_ref.1) | copy-start | bytes 98308
  0.0 10.3 %copy-start.3 = (bf16[32,1792]{1,0:T(8,128)(2,1)S(1)}, bf16[32,1792]{1,0:T(8,128)(2,1)}, u32[]{:S(2)}) copy-start(bf16[32,1792]{1,0:T(8,128)(2,1)} %left_ref.1) | copy-start | bytes 344068
  1.5 43.5 %collective-permute-start.2 = (bf16[384,2304]{1,0:T(8,128)(2,1)S(1)}, bf16[384,2304]{1,0:T(8,128)(2,1)S(1)}, u32[]{:S(2)}, u32[]{:S(2)}) collective-permute-start(bf16[384,2304]{1,0:T(8,128)(2,1)S(1)} %constant_dynamic-update-slice_fusion.refs_2_), channel_id=1, source_target_pairs={{0,16},{16,0},{1,17},{17,1},{2,18},{18,2},{3,19},{19,3},{4,20},{20... | collective-permute-start | bytes 5308424 | tf_op jit(solution)/shard_map/ppermute | solution.py:225
  45.0 0.8 copy-start.1
  45.0 1.0 copy-start.2
  47.9 1.2 %copy-start = (f32[16,8,3200]{2,1,0:T(8,128)}, f32[16,8,3200]{2,1,0:T(8,128)S(1)}, u32[]{:S(2)}) copy-start(f32[16,8,3200]{2,1,0:T(8,128)S(1)} %shard_map.47) | copy-start | bytes 4915204
  49.1 24.0 %all-to-all-start = ((f32[16,8,3200]{2,1,0:T(8,128)}), f32[16,8,3200]{2,1,0:T(8,128)}, u32[]{:S(2)}, u32[]{:S(2)}) async-start(f32[16,8,3200]{2,1,0:T(8,128)} %copy-done), calls=%async_computation | async-start | bytes 3276800 | tf_op jit(solution)/shard_map/all_to_all | solution.py:235
  55.6 13.4 %collective-permute-start.1 = (bf16[128,2432]{1,0:T(8,128)(2,1)}, bf16[128,2432]{1,0:T(8,128)(2,1)S(1)}, u32[]{:S(2)}, u32[]{:S(2)}) collective-permute-start(bf16[128,2432]{1,0:T(8,128)(2,1)} %copy-done.2), channel_id=1, source_target_pairs={{480,0},{0,32},{32,64},{64,96},{96,128},{128,160},{160,192},{192,2... | collective-permute-start | bytes 1867784 | tf_op jit(solution)/shard_map/ppermute | solution.py:222
  57.5 12.5 %collective-permute-start = (bf16[128,2432]{1,0:T(8,128)(2,1)}, bf16[128,2432]{1,0:T(8,128)(2,1)S(1)}, u32[]{:S(2)}, u32[]{:S(2)}) collective-permute-start(bf16[128,2432]{1,0:T(8,128)(2,1)} %copy-done.1), channel_id=1, source_target_pairs={{32,0},{64,32},{96,64},{128,96},{160,128},{192,160},{224,192},{256... | collective-permute-start | bytes 1867784 | tf_op jit(solution)/shard_map/ppermute | solution.py:222
  73.1 22.0 %all-to-all-start.1 = ((f32[16,8,3200]{2,1,0:T(8,128)}), f32[16,8,3200]{2,1,0:T(8,128)S(1)}, u32[]{:S(2)}, u32[]{:S(2)}) async-start(f32[16,8,3200]{2,1,0:T(8,128)} %shard_map.48), calls=%async_computation.1 | async-start | bytes 3276800 | tf_op jit(solution)/shard_map/all_to_all | solution.py:235
